TPU v7x, 128 devices: a whole 4x4x4 slice. The times are simulated.
128 devices in a mesh: span: 8 (over x_lo, y), seq: 16 (over x_hi, z, core).
Axes of the slice: x: 4 (x_hi: 2, x_lo: 2; x = x_hi * 2 + x_lo), y: 4, z: 4, core: 2. Of those that a mesh axis runs over, the one named last changes fastest.
Arguments:
- latent: bfloat16 [8, 1024, 5120], P('span', 'seq'), may hold values from -6 to 6
- noise: bfloat16 [8, 1024, 5120], P('span', 'seq'), may hold values from -6 to 6
- clean_keys: bfloat16 [8, 1024, 4096], P('span', None, 'seq'), may hold values from -256 to 256
- clean_values: bfloat16 [8, 1024, 4096], P('span', None, 'seq'), may hold values from -6 to 6
- w_query: bfloat16 [5120, 4096], P(None, 'seq'), may hold values from -0.078125 to 0.078125
- w_key: bfloat16 [5120, 4096], P(None, 'seq'), may hold values from -0.078125 to 0.078125
- w_value: bfloat16 [5120, 4096], P(None, 'seq'), may hold values from -0.078125 to 0.078125
- w_out: bfloat16 [4096, 5120], P('seq'), may hold values from -1.5 to 1.5
- modulation: float32 [8, 2, 5120], replicated, may hold values from -2 to 2
- plan: float32 [8, 2], replicated, may hold values from 0.15 to 1, as said below
- step_index: int32 [8], replicated, may hold values from 0 to 7
- assignment: int32 [8], replicated, may hold values from 0 to 7, each once
- visible: int32 [8, 8], replicated, may hold values from 0 to 1, as said below
Outputs:
- renoised: bfloat16 [8, 1024, 5120], P('span', 'seq')
Inputs may be any that keep to these rules, and one draw needn't show every extreme that they name: visible[c, j] is 1 only where j < c, and the row of span 8 - 1 is 1 at every j < 7. plan[i, 1] lies below plan[i, 0].
All inputs are finite; a program needn't handle non-finite values.
Results may differ from a plain program's by a relative error of at most 0.02.
Values may be sent and summed in bfloat16 or wider, within the bound.
A program may use at most 192 MiB of HBM per device.

v0:
```python
import jax
import jax.numpy as jnp
from jax import lax
from jax.sharding import PartitionSpec as P

HD = 128


def normalize(rows, shift, scale):
    values = rows.astype(jnp.float32)
    rms = lax.rsqrt(jnp.mean(values * values, axis=1, keepdims=True) + 1e-06)
    return (values * rms * (1.0 + scale) + shift).astype(jnp.bfloat16)


def local(
    latent,
    noise,
    clean_keys,
    clean_values,
    w_query,
    w_key,
    w_value,
    w_out,
    modulation,
    plan,
    step_index,
    assignment,
    visible,
):
    factor = 1.0 / HD**0.5
    count = step_index.shape[0]
    group = lax.axis_index("span")
    lanes = jnp.arange(count, dtype=jnp.int32)
    mine = (lanes == group).astype(jnp.int32)
    my_step = jnp.sum(step_index * mine)
    my_span = jnp.sum(assignment * mine)
    pick = (jnp.arange(modulation.shape[0], dtype=jnp.int32) == my_step).astype(jnp.float32)
    settings = jnp.sum(modulation * pick[:, None, None], axis=0)
    levels = jnp.sum(plan * pick[:, None], axis=0)
    level_now = levels[0]
    level_next = levels[1]
    row_pick = (lanes == my_span).astype(jnp.float32)
    seen_spans = jnp.sum(visible.astype(jnp.float32) * row_pick[:, None], axis=0)
    holder = (assignment[:, None] == lanes[None, :]).astype(jnp.float32)
    group_mask = jnp.sum(holder * seen_spans[None, :], axis=1)
    width = w_query.shape[1]
    heads_local = width // HD
    w_joined = jnp.concatenate((w_query, w_key, w_value), axis=1)
    normed = normalize(latent[0], settings[0], settings[1])
    joined = jnp.dot(
        lax.all_gather(normed, "seq", axis=0, tiled=True),
        w_joined,
        preferred_element_type=jnp.float32,
    ).astype(jnp.bfloat16)
    rows = joined.shape[0]
    query = joined[:, :width].reshape(rows, heads_local, HD)
    keys = joined[:, width : 2 * width].reshape(rows, heads_local, HD)
    values = joined[:, 2 * width :].reshape(rows, heads_local, HD)
    own = jnp.einsum("qhd,khd->hqk", query, keys, preferred_element_type=jnp.float32) * factor
    top = jnp.max(own, axis=2)
    weights = jnp.exp(own - top[:, :, None]).astype(jnp.bfloat16)
    total = jnp.sum(weights.astype(jnp.float32), axis=2)
    acc = jnp.einsum("hqk,khd->hqd", weights, values, preferred_element_type=jnp.float32)
    state = (top, total, acc)
    key_piece = lax.all_gather(clean_keys, "span", axis=0, tiled=True)
    value_piece = lax.all_gather(clean_values, "span", axis=0, tiled=True)
    for offset in range(key_piece.shape[0]):
        flag = lax.dynamic_slice_in_dim(group_mask, offset, 1, 0)[0]
        key_rows = key_piece[offset]
        value_rows = value_piece[offset]
        top_now, total_now, acc_now = state
        kpart = key_rows.reshape(key_rows.shape[0], heads_local, HD)
        vpart = value_rows.reshape(value_rows.shape[0], heads_local, HD)
        scores = (
            jnp.einsum("qhd,khd->hqk", query, kpart, preferred_element_type=jnp.float32) * factor
        )
        scores = jnp.where(flag > 0, scores, -jnp.inf)
        top_new = jnp.maximum(top_now, jnp.max(scores, axis=2))
        shrink = jnp.exp(top_now - top_new)
        block_weights = jnp.exp(scores - top_new[:, :, None]).astype(jnp.bfloat16)
        total_new = total_now * shrink + jnp.sum(block_weights.astype(jnp.float32), axis=2)
        acc_new = acc_now * shrink[:, :, None] + jnp.einsum(
            "hqk,khd->hqd", block_weights, vpart, preferred_element_type=jnp.float32
        )
        state = (top_new, total_new, acc_new)
    top, total, acc = state
    attended = (
        jnp.transpose(acc / total[:, :, None], (1, 0, 2)).reshape(rows, width).astype(jnp.bfloat16)
    )
    mixed = lax.psum_scatter(
        jnp.dot(attended, w_out, preferred_element_type=jnp.float32).astype(jnp.bfloat16),
        "seq",
        scatter_dimension=0,
        tiled=True,
    ).astype(jnp.float32)
    xrows = latent[0].astype(jnp.float32)
    result = (1.0 - level_next) * (xrows - level_now * (xrows + mixed)) + level_next * noise[
        0
    ].astype(jnp.float32)
    return result.astype(jnp.bfloat16)[None]


def solution(mesh):
    in_specs = (
        P("span", "seq", None),
        P("span", "seq", None),
        P("span", None, "seq"),
        P("span", None, "seq"),
        P(None, "seq"),
        P(None, "seq"),
        P(None, "seq"),
        P("seq", None),
        P(),
        P(),
        P(),
        P(),
        P(),
    )
    out_specs = P("span", "seq", None)
    return jax.shard_map(local, mesh=mesh, in_specs=in_specs, out_specs=out_specs, check_vma=False)
```

profile of v0, /device:TPU:1, one launch (start us, length us, event | category | flops | bytes accessed | tf_op | source)
XLA Modules:
  0.0 442.4 jit_solution(16962538457868069900)
XLA Ops:
  12.6 2.2 fusion.37
  22.7 42.1 %all-gather.6.cloned.1.call-done = bf16[8,1024,256]{2,1,0:T(8,128)(2,1)} async-done(((bf16[1,1024,256]{2,1,0:T(8,128)(2,1)}), bf16[8,1024,256]{2,1,0:T(8,128)(2,1)}) %all-gather.6.cloned.1.call-update) | async-done | bytes 4194320 | tf_op jit(solution)/shard_map/all_gather | solution.py:65
  64.8 4.0 fusion.77
  77.1 2.1 copy.195
  83.5 34.4 %all-gather.8.cloned.1.call-done = bf16[8,1024,256]{2,1,0:T(8,128)(2,1)} async-done(((bf16[1,1024,256]{2,1,0:T(8,128)(2,1)}), bf16[8,1024,256]{2,1,0:T(8,128)(2,1)}) %all-gather.8.cloned.1.call-update) | async-done | bytes 4194320 | tf_op jit(solution)/shard_map/all_gather | solution.py:66
  117.9 4.2 fusion.76
  128.2 2.1 copy.141
  130.3 2.1 copy.146
  138.6 63.0 %all-gather.4.cloned.1.call-done = bf16[1024,5120]{1,0:T(8,128)(2,1)} async-done(((bf16[64,5120]{1,0:T(8,128)(2,1)}), bf16[1024,5120]{1,0:T(8,128)(2,1)}) %all-gather.4.cloned.1.call-update) | async-done | bytes 10485776 | tf_op jit(solution)/shard_map/all_gather | solution.py:51
  201.7 14.0 %fusion.14 = bf16[1024,768]{0,1:T(8,128)(2,1)} fusion(bf16[1024,5120]{1,0:T(8,128)(2,1)} %all-gather.4.cloned.1.call-done, bf16[5120,256]{1,0:T(8,128)(2,1)} %param.19, bf16[5120,256]{1,0:T(8,128)(2,1)} %param.18, bf16[5120,256]{1,0:T(8,128)(2,1)} %param.17), kind=kOutput, calls=%fused_computation.46 | convolution fusion | flops 8077443072 | bytes 19922944 | tf_op jit(solution)/shard_map/dot_general | solution.py:50
  218.6 4.5 %fusion.8 = (f32[2,1024]{1,0:T(2,128)S(1)}, f32[2,1024,1024]{1,2,0:T(8,128)}) fusion(pred[]{:T(512)} %bitcast.21, bf16[1024,2,128]{0,2,1:T(8,128)(2,1)S(1)} %bitcast.256, bf16[1024,2,128]{0,2,1:T(8,128)(2,1)S(1)} %bitcast.275), kind=kOutput, calls=%fused_computation.36 | convolution fusion | flops 543160320 | bytes 9445377 | tf_op jit(solution)/shard_map/qhd,khd->hqk/dot_general | solution.py:75
  223.1 4.5 %fusion.6 = (f32[2,1024]{1,0:T(2,128)S(1)}, f32[2,1024,1024]{1,2,0:T(8,128)}) fusion(pred[]{:T(512)} %bitcast.11, bf16[1024,2,128]{0,2,1:T(8,128)(2,1)S(1)} %bitcast.257, bf16[1024,2,128]{0,2,1:T(8,128)(2,1)S(1)} %bitcast.274), kind=kOutput, calls=%fused_computation.34 | convolution fusion | flops 543160320 | bytes 9445377 | tf_op jit(solution)/shard_map/qhd,khd->hqk/dot_general | solution.py:75
  230.3 4.5 %fusion.11 = (f32[2,1024]{1,0:T(2,128)S(1)}, f32[2,1024,1024]{1,2,0:T(8,128)}) fusion(pred[]{:T(512)} %bitcast.36, bf16[1024,2,128]{0,2,1:T(8,128)(2,1)S(1)} %bitcast.260, bf16[1024,2,128]{0,2,1:T(8,128)(2,1)S(1)} %bitcast.271), kind=kOutput, calls=%fused_computation.39 | convolution fusion | flops 543160320 | bytes 9445377 | tf_op jit(solution)/shard_map/qhd,khd->hqk/dot_general | solution.py:75
  234.8 4.5 %fusion.10 = (f32[2,1024]{1,0:T(2,128)S(1)}, f32[2,1024,1024]{1,2,0:T(8,128)}) fusion(pred[]{:T(512)} %bitcast.31, bf16[1024,2,128]{0,2,1:T(8,128)(2,1)S(1)} %bitcast.261, bf16[1024,2,128]{0,2,1:T(8,128)(2,1)S(1)} %bitcast.270), kind=kOutput, calls=%fused_computation.38 | convolution fusion | flops 543160320 | bytes 9445377 | tf_op jit(solution)/shard_map/qhd,khd->hqk/dot_general | solution.py:75
  239.3 4.5 %fusion.9 = (f32[2,1024]{1,0:T(2,128)S(1)}, f32[2,1024,1024]{1,2,0:T(8,128)}) fusion(pred[]{:T(512)} %bitcast.26, bf16[1024,2,128]{0,2,1:T(8,128)(2,1)S(1)} %bitcast.262, bf16[1024,2,128]{0,2,1:T(8,128)(2,1)S(1)} %bitcast.269), kind=kOutput, calls=%fused_computation.37 | convolution fusion | flops 543160320 | bytes 9445377 | tf_op jit(solution)/shard_map/qhd,khd->hqk/dot_general | solution.py:75
  243.9 4.5 %fusion.7 = (f32[2,1024]{1,0:T(2,128)S(1)}, f32[2,1024,1024]{1,2,0:T(8,128)}) fusion(pred[]{:T(512)} %bitcast.16, bf16[1024,2,128]{0,2,1:T(8,128)(2,1)S(1)} %bitcast.263, bf16[1024,2,128]{0,2,1:T(8,128)(2,1)S(1)} %bitcast.268), kind=kOutput, calls=%fused_computation.35 | convolution fusion | flops 543160320 | bytes 9445377 | tf_op jit(solution)/shard_map/qhd,khd->hqk/dot_general | solution.py:75
  250.0 5.0 %convert_reduce_fusion.7 = f32[2,1024]{1,0:T(2,128)S(1)} fusion(f32[2,1024]{1,0:T(2,128)S(1)} %get-tuple-element.21, f32[2,1024,1024]{1,2,0:T(8,128)} %get-tuple-element.72, pred[]{:T(512)} %bitcast.11), kind=kLoop, calls=%fused_computation.8 | loop fusion | flops 12580864 | bytes 8404993 | tf_op jit(solution)/shard_map/reduce_sum | solution.py:81
  255.0 5.0 %convert_reduce_fusion.6 = f32[2,1024]{1,0:T(2,128)S(1)} fusion(f32[2,1024]{1,0:T(2,128)S(1)} %get-tuple-element.20, f32[2,1024,1024]{1,2,0:T(8,128)} %get-tuple-element.70, pred[]{:T(512)} %bitcast.16), kind=kLoop, calls=%fused_computation.7 | loop fusion | flops 12580864 | bytes 8404993 | tf_op jit(solution)/shard_map/reduce_sum | solution.py:81
  260.0 5.0 %convert_reduce_fusion.5 = f32[2,1024]{1,0:T(2,128)S(1)} fusion(f32[2,1024]{1,0:T(2,128)S(1)} %get-tuple-element.19, f32[2,1024,1024]{1,2,0:T(8,128)} %get-tuple-element.68, pred[]{:T(512)} %bitcast.21), kind=kLoop, calls=%fused_computation.6 | loop fusion | flops 12580864 | bytes 8404993 | tf_op jit(solution)/shard_map/reduce_sum | solution.py:81
  265.1 5.0 %convert_reduce_fusion.4 = f32[2,1024]{1,0:T(2,128)S(1)} fusion(f32[2,1024]{1,0:T(2,128)S(1)} %get-tuple-element.18, f32[2,1024,1024]{1,2,0:T(8,128)} %get-tuple-element.66, pred[]{:T(512)} %bitcast.26), kind=kLoop, calls=%fused_computation.5 | loop fusion | flops 12580864 | bytes 8404993 | tf_op jit(solution)/shard_map/reduce_sum | solution.py:81
  270.1 5.0 %convert_reduce_fusion.3 = f32[2,1024]{1,0:T(2,128)S(1)} fusion(f32[2,1024]{1,0:T(2,128)S(1)} %get-tuple-element.17, f32[2,1024,1024]{1,2,0:T(8,128)} %get-tuple-element.64, pred[]{:T(512)} %bitcast.31), kind=kLoop, calls=%fused_computation.4 | loop fusion | flops 12580864 | bytes 8404993 | tf_op jit(solution)/shard_map/reduce_sum | solution.py:81
  275.1 5.0 %convert_reduce_fusion.2 = f32[2,1024]{1,0:T(2,128)S(1)} fusion(f32[2,1024]{1,0:T(2,128)S(1)} %get-tuple-element.16, f32[2,1024,1024]{1,2,0:T(8,128)} %get-tuple-element.62, pred[]{:T(512)} %bitcast.36), kind=kLoop, calls=%fused_computation.3 | loop fusion | flops 12580864 | bytes 8404993 | tf_op jit(solution)/shard_map/reduce_sum | solution.py:81
  285.4 5.6 %fusion.31 = f32[1024,2,128]{0,2,1:T(8,128)S(1)} fusion(f32[1024,2,128]{0,2,1:T(8,128)S(1)} %fusion.32, bf16[1024,2,128]{0,2,1:T(8,128)(2,1)S(1)} %bitcast.285, f32[1024,2]{0,1:T(2,128)S(1)} %get-tuple-element.12, f32[2,1024,1024]{1,2,0:T(8,128)} %get-tuple-element.72, f32[2,1024]{1,0:T(2,128)S(1)} %get-tuple-element.21, pred[]{:T(512)} %bitcast.11), kind=kOutput, calls=%fused_computation.69 | convolution fusion | flops 545783808 | bytes 11026433 | tf_op jit(solution)/shard_map/hqk,khd->hqd/dot_general | solution.py:82
  291.1 5.5 %fusion.29 = f32[1024,2,128]{0,2,1:T(8,128)S(1)} fusion(f32[1024,2,128]{0,2,1:T(8,128)S(1)} %fusion.31, bf16[1024,2,128]{0,2,1:T(8,128)(2,1)S(1)} %bitcast.284, f32[1024,2]{0,1:T(2,128)S(1)} %get-tuple-element.11, f32[2,1024,1024]{1,2,0:T(8,128)} %get-tuple-element.70, f32[2,1024]{1,0:T(2,128)S(1)} %get-tuple-element.20, pred[]{:T(512)} %bitcast.16), kind=kOutput, calls=%fused_computation.66 | convolution fusion | flops 545783808 | bytes 11026433 | tf_op jit(solution)/shard_map/hqk,khd->hqd/dot_general | solution.py:82
  296.7 2.5 fusion.27
  299.2 5.6 %fusion.25 = f32[1024,2,128]{0,2,1:T(8,128)S(1)} fusion(f32[1024,2,128]{0,2,1:T(8,128)S(1)} %fusion.27, bf16[1024,2,128]{0,2,1:T(8,128)(2,1)S(1)} %bitcast.282, f32[1024,2]{0,1:T(2,128)S(1)} %get-tuple-element.9, f32[2,1024,1024]{1,2,0:T(8,128)} %get-tuple-element.66, f32[2,1024]{1,0:T(2,128)S(1)} %get-tuple-element.18, pred[]{:T(512)} %bitcast.26), kind=kOutput, calls=%fused_computation.60 | convolution fusion | flops 545783808 | bytes 11026433 | tf_op jit(solution)/shard_map/hqk,khd->hqd/dot_general | solution.py:82
  304.8 5.6 %fusion.23 = f32[1024,2,128]{0,2,1:T(8,128)S(1)} fusion(f32[1024,2,128]{0,2,1:T(8,128)S(1)} %fusion.25, bf16[1024,2,128]{0,2,1:T(8,128)(2,1)S(1)} %bitcast.281, f32[1024,2]{0,1:T(2,128)S(1)} %get-tuple-element.8, f32[2,1024,1024]{1,2,0:T(8,128)} %get-tuple-element.64, f32[2,1024]{1,0:T(2,128)S(1)} %get-tuple-element.17, pred[]{:T(512)} %bitcast.31), kind=kOutput, calls=%fused_computation.57 | convolution fusion | flops 545783808 | bytes 11026433 | tf_op jit(solution)/shard_map/hqk,khd->hqd/dot_general | solution.py:82
  310.4 2.3 fusion.21
  312.7 2.2 fusion.19
  317.0 5.5 %convolution_convert_fusion = bf16[1024,5120]{1,0:T(8,128)(2,1)} fusion(bf16[1024,256]{0,1:T(8,128)(2,1)S(1)} %bitcast.286, bf16[256,5120]{1,0:T(8,128)(2,1)S(1)} %copy-done), kind=kOutput, calls=%fused_computation | convolution fusion | flops 2689597440 | bytes 13631488 | tf_op jit(solution)/shard_map/dot_general | solution.py:91
  324.7 106.9 %reduce-scatter.2.cloned.1.call-done = bf16[64,5120]{1,0:T(8,128)(2,1)} async-done(((bf16[1024,5120]{1,0:T(8,128)(2,1)}), bf16[64,5120]{1,0:T(8,128)(2,1)}) %reduce-scatter.2.cloned.1.call-update) | async-done | bytes 655376 | tf_op jit(solution)/shard_map/reduce_scatter | solution.py:90
  431.6 3.8 fusion.43
  (91 shorter events, 49.6 us)
Async XLA Ops:
  6.5 310.5 %copy-start = (bf16[256,5120]{1,0:T(8,128)(2,1)S(1)}, bf16[256,5120]{1,0:T(8,128)(2,1)}, u32[]{:S(2)}) copy-start(bf16[256,5120]{1,0:T(8,128)(2,1)} %param.20) | copy-start | bytes 7864324
  6.5 58.3 %all-gather.6.cloned.1.call-start = ((), (), s32[]{:S(2)}) async-start(), calls=%async_computation.2 | async-start | bytes 4718592 | tf_op jit(solution)/shard_map/all_gather | solution.py:65
  7.3 110.7 %all-gather.8.cloned.1.call-start = ((), (), s32[]{:S(2)}) async-start(), calls=%async_computation.3 | async-start | bytes 4718592 | tf_op jit(solution)/shard_map/all_gather | solution.py:66
  8.0 193.6 %all-gather.4.cloned.1.call-start = ((), (), s32[]{:S(2)}) async-start(), calls=%async_computation.1 | async-start | bytes 11141120 | tf_op jit(solution)/shard_map/all_gather | solution.py:51
  14.9 416.7 %reduce-scatter.2.cloned.1.call-start = ((), (), s32[]{:S(2)}) async-start(), calls=%async_computation.4 | async-start | bytes 11141120 | tf_op jit(solution)/shard_map/reduce_scatter | solution.py:90
  215.7 2.9 copy-start.8
  217.2 5.9 %copy-start.7 = (bf16[1,1024,256]{1,2,0:T(8,128)(2,1)S(1)}, bf16[1,1024,256]{1,2,0:T(8,128)(2,1)}, u32[]{:S(2)}) copy-start(bf16[1,1024,256]{1,2,0:T(8,128)(2,1)} %copy.190) | copy-start | bytes 1572868
  218.6 9.0 %copy-start.6 = (bf16[1,1024,256]{1,2,0:T(8,128)(2,1)S(1)}, bf16[1,1024,256]{1,2,0:T(8,128)(2,1)}, u32[]{:S(2)}) copy-start(bf16[1,1024,256]{1,2,0:T(8,128)(2,1)} %copy.197) | copy-start | bytes 1572868
  223.1 5.8 %copy-start.5 = (bf16[1,1024,256]{1,2,0:T(8,128)(2,1)S(1)}, bf16[1,1024,256]{1,2,0:T(8,128)(2,1)}, u32[]{:S(2)}) copy-start(bf16[1,1024,256]{1,2,0:T(8,128)(2,1)} %copy.196) | copy-start | bytes 1572868
  227.6 2.7 copy-start.4
  228.9 5.9 %copy-start.3 = (bf16[1,1024,256]{1,2,0:T(8,128)(2,1)S(1)}, bf16[1,1024,256]{1,2,0:T(8,128)(2,1)}, u32[]{:S(2)}) copy-start(bf16[1,1024,256]{1,2,0:T(8,128)(2,1)} %copy.194) | copy-start | bytes 1572868
  230.3 9.1 %copy-start.2 = (bf16[1,1024,256]{1,2,0:T(8,128)(2,1)S(1)}, bf16[1,1024,256]{1,2,0:T(8,128)(2,1)}, u32[]{:S(2)}) copy-start(bf16[1,1024,256]{1,2,0:T(8,128)(2,1)} %copy.193) | copy-start | bytes 1572868
  282.0 3.4 copy-start.16
  285.4 5.6 %copy-start.15 = (bf16[1,1024,256]{1,2,0:T(8,128)(2,1)S(1)}, bf16[1,1024,256]{1,2,0:T(8,128)(2,1)}, u32[]{:S(2)}) copy-start(bf16[1,1024,256]{1,2,0:T(8,128)(2,1)} %copy.131) | copy-start | bytes 1572868
  285.4 11.2 %slice-start.2 = ((s8[8388608]{0:T(1024)(128)(4,1)}), s8[4194304]{0:T(1024)(128)(4,1)S(1)}, s32[]{:S(2)}) async-start(s8[8388608]{0:T(1024)(128)(4,1)} %bitcast.266), calls=%async_computation.7 | async-start | bytes 8388608
  291.1 5.6 %copy-start.14 = (bf16[1,1024,256]{1,2,0:T(8,128)(2,1)S(1)}, bf16[1,1024,256]{1,2,0:T(8,128)(2,1)}, u32[]{:S(2)}) copy-start(bf16[1,1024,256]{1,2,0:T(8,128)(2,1)} %copy.136) | copy-start | bytes 1572868
  291.1 5.6 %slice-start.3 = ((s8[8388608]{0:T(1024)(128)(4,1)}), s8[4194304]{0:T(1024)(128)(4,1)S(1)}, s32[]{:S(2)}) async-start(s8[8388608]{0:T(1024)(128)(4,1)} %bitcast.266), calls=%async_computation.8 | async-start | bytes 8388608
  296.6 2.6 copy-start.13
  299.2 5.6 %copy-start.12 = (bf16[1,1024,256]{1,2,0:T(8,128)(2,1)S(1)}, bf16[1,1024,256]{1,2,0:T(8,128)(2,1)}, u32[]{:S(2)}) copy-start(bf16[1,1024,256]{1,2,0:T(8,128)(2,1)} %copy.146) | copy-start | bytes 1572868
  299.2 11.2 %slice-start = ((s8[8388608]{0:T(1024)(128)(4,1)}), s8[4194304]{0:T(1024)(128)(4,1)S(1)}, s32[]{:S(2)}) async-start(s8[8388608]{0:T(1024)(128)(4,1)} %bitcast.264), calls=%async_computation.5 | async-start | bytes 8388608
  304.8 5.6 %copy-start.11 = (bf16[1,1024,256]{1,2,0:T(8,128)(2,1)S(1)}, bf16[1,1024,256]{1,2,0:T(8,128)(2,1)}, u32[]{:S(2)}) copy-start(bf16[1,1024,256]{1,2,0:T(8,128)(2,1)} %copy.151) | copy-start | bytes 1572868
  304.8 5.6 %slice-start.1 = ((s8[8388608]{0:T(1024)(128)(4,1)}), s8[4194304]{0:T(1024)(128)(4,1)S(1)}, s32[]{:S(2)}) async-start(s8[8388608]{0:T(1024)(128)(4,1)} %bitcast.264), calls=%async_computation.6 | async-start | bytes 8388608
  310.4 2.3 copy-start.10
  312.7 2.3 copy-start.9
  322.5 0.7 copy-start.17
  322.5 109.1 %copy-start.1 = (bf16[1,64,5120]{2,1,0:T(8,128)(2,1)S(1)}, bf16[1,64,5120]{2,1,0:T(8,128)(2,1)}, u32[]{:S(2)}) copy-start(bf16[1,64,5120]{2,1,0:T(8,128)(2,1)} %param.13) | copy-start | bytes 1966084
Sparse Core Ops, SparseCore 0:
  9.0 55.7 all-gather.5
  66.5 51.3 all-gather.7
  120.4 81.2 all-gather.3
  322.7 108.8 reduce-scatter.1
where the time goes:
time: 451 us; the launch traced here: 442 us
  waiting for transfers between devices  248 us (55%)
  matrix products  83.5 us (19%)
  other arithmetic  48.3 us (11%)
  local copies, waits for them, and re-layouts  42.9 us (10%)
  between operations  19.6 us (4%)
    reduce_scatter x1, waiting for transfers between devices, local(): lax.psum_scatter(jnp.dot(attended, w_out, preferred_element_type=jnp.floa...  107 us
    all_gather x1, waiting for transfers between devices, local(): lax.all_gather(normed, 'seq', axis=0, tiled=True)  63 us
    all_gather x1, waiting for transfers between devices, local(): key_piece = lax.all_gather(clean_keys, 'span', axis=0, tiled=True)  42.1 us
    all_gather x1, waiting for transfers between devices, local(): value_piece = lax.all_gather(clean_values, 'span', axis=0, tiled=True)  34.4 us
    reduce_sum x8, other arithmetic, local(): jnp.sum(block_weights.astype(jnp.float32), axis=2)  33.7 us
    dot_general x8, matrix products, local(): jnp.einsum('hqk,khd->hqd', block_weights, vpart, preferred_element_type=j...  31.3 us
    dot_general x8, matrix products, local(): jnp.einsum('qhd,khd->hqk', query, kpart, preferred_element_type=jnp.float32)  29.7 us
    slice x9, local copies, waits for them, and re-layouts, local(): value_rows = value_piece[offset]  20.7 us
  transfers between devices with their start and end apart: 4, of which 4 were waited for; matrix products, arithmetic and copies ran while one was open for 11% of the time, Pallas kernels for 0%

commit v1 on v0

v1 whole, which is shorter than its diff:
```python
import jax
import jax.numpy as jnp
from jax import lax
from jax.experimental import pallas as pl
from jax.experimental.pallas import tpu as pltpu
from jax.sharding import PartitionSpec as P

HD = 128
D = 5120
TOK = 1024
W = 256
ROWS = 64
HALF = 32
GROUP = 256
PIECE = 256
LOG2E = 1.4426950408889634
SCALE = LOG2E / HD**0.5
LOW = -1e30
HIGH = 3e38
MESH = pl.DeviceIdType.MESH
N_SEM = 144

PLACE = {(0, 0): 0, (1, 0): 1, (0, 1): 2, (0, 3): 3, (1, 1): 4, (1, 3): 5, (0, 2): 6, (1, 2): 7}
CACHE = {(0, 0): 0, (0, 1): 1, (0, 3): 2, (1, 0): 3, (1, 1): 4, (1, 3): 5, (0, 2): 6, (1, 2): 7}
OWN = 8
A, B, C, E = 0, 1, 2, 3


def kernel(
    latent_hbm,
    noise_hbm,
    ck_hbm,
    cv_hbm,
    wq_hbm,
    wk_hbm,
    wv_hbm,
    wo_hbm,
    modulation,
    plan,
    step_index,
    assignment,
    visible,
    out,
    lat,
    noise,
    w,
    wo,
    g,
    kv,
    q,
    acc,
    top,
    att,
    p0,
    p1,
    s,
    r1,
    r2,
    xb,
    flags,
    local_sem,
    send_sem,
    recv_sem,
):
    span = lax.axis_index("span")
    seq = lax.axis_index("seq")
    x_lo = span // 4
    y = span % 4
    x_hi = seq // 8
    z = (seq // 2) % 4
    core = seq % 2

    def seq_of(a, b, c):
        return a * 8 + b * 2 + c

    sib = (span, seq_of(x_hi, z, 1 - core))
    x2 = (span, seq_of(1 - x_hi, z, core))
    zp = (span, seq_of(x_hi, (z + 1) % 4, core))
    zm = (span, seq_of(x_hi, (z + 3) % 4, core))
    xn = ((1 - x_lo) * 4 + y, seq)
    yp = (x_lo * 4 + (y + 1) % 4, seq)
    ym = (x_lo * 4 + (y + 3) % 4, seq)

    loads = {}
    for i, (name, src, dst) in enumerate(
        (
            ("k", ck_hbm.at[0], kv.at[0, 0]),
            ("v", cv_hbm.at[0], kv.at[0, 1]),
            ("lat", latent_hbm.at[0], lat),
            ("wq", wq_hbm, w.at[0]),
            ("wk", wk_hbm, w.at[1]),
            ("wv", wv_hbm, w.at[2]),
            ("wo", wo_hbm, wo),
            ("noise", noise_hbm.at[0], noise),
        )
    ):
        loads[name] = pltpu.make_async_copy(src, dst, local_sem.at[i])
        loads[name].start()

    barrier = pltpu.get_barrier_semaphore()
    for device in (sib, x2, zp, zm, xn, yp, ym):
        pl.semaphore_signal(barrier, 1, device_id=device, device_id_type=MESH)
    pl.semaphore_wait(barrier, 7)

    started = []

    def send(src, dst, device):
        i = len(started)
        copy = pltpu.make_async_remote_copy(
            src, dst, send_sem.at[i], recv_sem.at[i], device_id=device, device_id_type=MESH
        )
        copy.start()
        started.append(copy)
        return copy

    def piece(place, j):
        return kv.at[place, :, pl.ds(j * PIECE, PIECE)]

    def part(place, side, j):
        return kv.at[place, side, pl.ds(j * PIECE, PIECE)]

    def send_piece(src, dst, j, device):
        return send(piece(CACHE[src], j), piece(CACHE[dst], j), device)

    loads["k"].wait()
    loads["v"].wait()
    y_up, y_down, x_over = {}, {}, {}
    for j in range(4):
        y_up[0, j] = send_piece((0, 0), (0, 3), j, yp)
        y_down[0, j] = send_piece((0, 0), (0, 1), j, ym)
    x_over[0, 0] = send_piece((0, 0), (1, 0), 0, xn)

    def rows_of(place, sub, half=None):
        base = PLACE[place] * 2 * ROWS + sub * ROWS
        if half is None:
            return g.at[pl.ds(base, ROWS)]
        return g.at[pl.ds(base + half * HALF, HALF)]

    step = step_index[span]
    level_now = plan[step, 0]
    level_next = plan[step, 1]
    loads["lat"].wait()

    @pl.loop(0, 4)
    def _(i):
        rows = pl.ds(pl.multiple_of(i * 16, 16), 16)
        values = lat[rows, :].astype(jnp.float32)
        rms = lax.rsqrt(jnp.mean(values * values, axis=1, keepdims=True) + 1e-06)
        shift = modulation[step, 0:1, :]
        scale = modulation[step, 1:2, :]
        g[rows, :] = (values * rms * (1.0 + scale) + shift).astype(jnp.bfloat16)

    x_part, z_up, z_down, over = {}, {}, {}, {}
    for h in range(2):
        x_part[h] = send(rows_of((0, 0), 0, h), rows_of((1, 0), 0, h), x2)
    for h in range(2):
        z_up[0, h] = send(rows_of((0, 0), 0, h), rows_of((0, 3), 0, h), zp)
        z_down[0, h] = send(rows_of((0, 0), 0, h), rows_of((0, 1), 0, h), zm)

    def to_sibling(place):
        over[place] = send(rows_of(place, 0), rows_of(place, 1), sib)

    to_sibling((0, 0))

    mine = assignment[span]
    for (dx, dy), place in CACHE.items():
        other = ((x_lo + dx) % 2) * 4 + (y + dy) % 4
        flags[place] = visible[mine, assignment[other]]
    flags[OWN] = 1

    acc[...] = jnp.zeros_like(acc)
    top[...] = jnp.full_like(top, LOW)

    for h in range(2):
        x_part[h].wait_recv()
        z_up[1, h] = send(rows_of((1, 0), 0, h), rows_of((1, 3), 0, h), zp)
        z_down[1, h] = send(rows_of((1, 0), 0, h), rows_of((1, 1), 0, h), zm)
    to_sibling((1, 0))
    for j in (1, 2):
        x_over[0, j] = send_piece((0, 0), (1, 0), j, xn)

    def project(group):
        rows = pl.ds(group * GROUP, GROUP)

        @pl.loop(0, 3)
        def _(i):
            y = jnp.dot(g[rows, :], w[i], preferred_element_type=jnp.float32).astype(jnp.bfloat16)

            @pl.when(i == 0)
            def _():
                q[rows, :] = y

            @pl.when(i > 0)
            def _():
                kv[OWN, i - 1, rows, :] = y

    ones = jnp.ones((TOK, HD), jnp.bfloat16)

    def attend(group, place):
        rows = pl.ds(pl.multiple_of(group * GROUP, GROUP), GROUP)
        seen = jnp.full((GROUP, HD), flags[place], jnp.int32) > 0
        for h in range(W // HD):
            cols = slice(h * HD, (h + 1) * HD)
            scores = lax.dot_general(
                q[rows, cols],
                kv[place, 0, :, cols],
                (((1,), (1,)), ((), ())),
                preferred_element_type=jnp.float32,
            )
            old = top[rows, cols]
            peak = jnp.max(scores, axis=1, keepdims=True) * SCALE
            new = jnp.where(seen, jnp.maximum(old, peak), old)
            low = jnp.where(seen, new, HIGH)
            weights = jnp.exp2(scores * SCALE - jnp.tile(low, (1, TOK // HD))).astype(jnp.bfloat16)
            both = jnp.concatenate((kv[place, 1, :, cols], ones), axis=1)
            sums = jnp.dot(weights, both, preferred_element_type=jnp.float32)
            shrink = jnp.exp2(old - new)
            wide = slice(h * 2 * HD, (h + 1) * 2 * HD)
            acc[rows, wide] = acc[rows, wide] * jnp.tile(shrink, (1, 2)) + sums
            top[rows, cols] = new

    def attend_all(first_group, last_group, first_place, last_place):
        groups = last_group - first_group + 1

        @pl.loop(0, groups * (last_place - first_place + 1))
        def _(i):
            attend(first_group + i % groups, first_place + i // groups)

    for name in ("wq", "wk", "wv"):
        loads[name].wait()
    x_over[0, 0].wait_recv()
    y_up[1, 0] = send_piece((1, 0), (1, 3), 0, yp)
    y_down[1, 0] = send_piece((1, 0), (1, 1), 0, ym)
    over[0, 0].wait_recv()
    over[1, 0].wait_recv()
    project(A)

    z_fwd_up, z_fwd_down = {}, {}

    def forward_z(x):
        for h in range(2):
            z_up[x, h].wait_recv()
            z_down[x, h].wait_recv()
        z_fwd_up[x] = send(rows_of((x, 3), 0, 0), rows_of((x, 2), 0, 0), zp)
        z_fwd_down[x] = send(rows_of((x, 1), 0, 1), rows_of((x, 2), 0, 1), zm)
        to_sibling((x, 3))
        to_sibling((x, 1))

    forward_z(0)
    over[0, 1].wait_recv()
    over[0, 3].wait_recv()
    project(B)
    attend_all(A, B, 0, 0)
    for j in range(4):
        y_up[0, j].wait_recv()
        y_down[0, j].wait_recv()
    attend_all(A, B, 1, 2)
    forward_z(1)
    for j in (1, 2):
        x_over[0, j].wait_recv()
        y_up[1, j] = send_piece((1, 0), (1, 3), j, yp)
        y_down[1, j] = send_piece((1, 0), (1, 1), j, ym)
    y_fwd_up, y_fwd_down = {}, {}

    def forward_y(x, j):
        y_fwd_up[x, j] = send(part(CACHE[x, 3], 0, j), part(CACHE[x, 2], 0, j), yp)
        y_fwd_down[x, j] = send(part(CACHE[x, 1], 1, j), part(CACHE[x, 2], 1, j), ym)

    for j in (3, 0, 1, 2):
        forward_y(0, j)
    for dy in (0, 1, 3):
        x_over[dy, 3] = send_piece((0, dy), (1, dy), 3, xn)
    over[1, 1].wait_recv()
    over[1, 3].wait_recv()
    project(C)
    attend_all(C, C, 0, 2)
    for x in range(2):
        z_fwd_up[x].wait_recv()
        z_fwd_down[x].wait_recv()
        to_sibling((x, 2))
    x_over[0, 3].wait_recv()
    attend_all(A, C, 3, 3)
    for j in range(3):
        y_up[1, j].wait_recv()
        y_down[1, j].wait_recv()
        forward_y(1, j)
    y_fwd_up[0, 3].wait_recv()
    y_fwd_down[0, 3].wait_recv()
    x_over[2, 3] = send_piece((0, 2), (1, 2), 3, xn)
    over[0, 2].wait_recv()
    over[1, 2].wait_recv()
    project(E)
    attend_all(E, E, 0, 3)
    attend_all(A, E, OWN, OWN)
    x_over[1, 3].wait_recv()
    x_over[3, 3].wait_recv()
    attend_all(A, E, 4, 5)
    for j in range(3):
        y_fwd_up[0, j].wait_recv()
        y_fwd_down[0, j].wait_recv()
    for j in range(3):
        y_fwd_up[1, j].wait_recv()
        y_fwd_down[1, j].wait_recv()
    x_over[2, 3].wait_recv()
    loads["wo"].wait()
    loads["noise"].wait()

    part_over = {}

    def finish(group):
        attend_all(group, group, 6, 7)
        rows = pl.ds(group * GROUP, GROUP)
        for h in range(W // HD):
            lead = h * 2 * HD
            att[:, h * HD : (h + 1) * HD] = (
                acc[rows, lead : lead + HD] / acc[rows, lead + HD : lead + 2 * HD]
            ).astype(jnp.bfloat16)

        @pl.loop(0, 10)
        def _(i):
            cols = pl.ds(pl.multiple_of(i * 512, 512), 512)
            y = jnp.dot(att[...], wo[:, cols], preferred_element_type=jnp.float32)
            y = y.astype(jnp.bfloat16)
            p0[2 * group, :, cols] = y[:ROWS]
            p1[2 * group, :, cols] = y[ROWS : 2 * ROWS]
            p0[2 * group + 1, :, cols] = y[2 * ROWS : 3 * ROWS]
            p1[2 * group + 1, :, cols] = y[3 * ROWS :]

        for place in (2 * group + 1, 2 * group):
            part_over[place] = send(p1.at[place], s.at[place], sib)

    def total(dst, *terms):
        count = dst.shape[0] // 16

        @pl.loop(0, count)
        def _(i):
            rows = pl.ds(pl.multiple_of(i * 16, 16), 16)
            value = terms[0][rows, :].astype(jnp.float32)
            for term in terms[1:]:
                value = value + term[rows, :].astype(jnp.float32)
            dst[rows, :] = value.astype(jnp.bfloat16)

    half_rows = (pl.ds(0, HALF), pl.ds(HALF, HALF))
    r1_up, r1_down, r2_up, r2_down = {}, {}, {}, {}

    def first_hop(x):
        place = PLACE[x, 2]
        part_over[place].wait_recv()
        total(p0.at[place], p0.at[place], s.at[place])
        r1_up[x] = send(p0.at[place, half_rows[0]], r1.at[x, 0], zp)
        r1_down[x] = send(p0.at[place, half_rows[1]], r1.at[x, 1], zm)

    def second_hop(x):
        up, down = PLACE[x, 1], PLACE[x, 3]
        part_over[up].wait_recv()
        part_over[down].wait_recv()
        a, b = half_rows
        total(p0.at[up, b], p0.at[up, b], s.at[up, b])
        r2_up[x, 1] = send(p0.at[up, b], r2.at[x, 0, b], zp)
        total(p0.at[down, a], p0.at[down, a], s.at[down, a])
        r2_down[x, 0] = send(p0.at[down, a], r2.at[x, 1, a], zm)
        r1_up[x].wait_recv()
        total(p0.at[up, a], p0.at[up, a], s.at[up, a], r1.at[x, 0])
        r2_up[x, 0] = send(p0.at[up, a], r2.at[x, 0, a], zp)
        r1_down[x].wait_recv()
        total(p0.at[down, b], p0.at[down, b], s.at[down, b], r1.at[x, 1])
        r2_down[x, 1] = send(p0.at[down, b], r2.at[x, 1, b], zm)

    finish(E)
    finish(C)
    first_hop(1)
    first_hop(0)
    finish(B)
    finish(A)
    second_hop(1)
    second_hop(0)
    part_over[1].wait_recv()
    last = {}
    for h, rows in ((0, half_rows[0]), (1, half_rows[1])):
        r2_up[1, h].wait_recv()
        r2_down[1, h].wait_recv()
        total(p0.at[1, rows], p0.at[1, rows], s.at[1, rows], r2.at[1, 0, rows], r2.at[1, 1, rows])
        last[h] = send(p0.at[1, rows], xb.at[rows], x2)
    part_over[0].wait_recv()
    for h in range(2):
        r2_up[0, h].wait_recv()
        r2_down[0, h].wait_recv()
        last[h].wait_recv()

    @pl.loop(0, 4)
    def _(i):
        rows = pl.ds(pl.multiple_of(i * 16, 16), 16)
        mixed = p0[0, rows, :].astype(jnp.float32) + s[0, rows, :].astype(jnp.float32)
        mixed = mixed + r2[0, 0, rows, :].astype(jnp.float32) + r2[0, 1, rows, :].astype(jnp.float32)
        mixed = mixed + xb[rows, :].astype(jnp.float32)
        xrows = lat[rows, :].astype(jnp.float32)
        fresh = noise[rows, :].astype(jnp.float32)
        result = (1.0 - level_next) * (xrows - level_now * (xrows + mixed)) + level_next * fresh
        out[0, rows, :] = result.astype(jnp.bfloat16)

    for copy in started:
        copy.wait_send()


def local(*operands):
    bf16, f32 = jnp.bfloat16, jnp.float32
    anywhere = pl.BlockSpec(memory_space=pl.ANY)
    vmem = pl.BlockSpec(memory_space=pltpu.VMEM)
    smem = pl.BlockSpec(memory_space=pltpu.SMEM)
    return pl.pallas_call(
        kernel,
        out_shape=jax.ShapeDtypeStruct((1, ROWS, D), bf16),
        in_specs=[anywhere] * 8 + [vmem] + [smem] * 4,
        out_specs=vmem,
        scratch_shapes=[
            pltpu.VMEM((ROWS, D), bf16),
            pltpu.VMEM((ROWS, D), bf16),
            pltpu.VMEM((3, D, W), bf16),
            pltpu.VMEM((W, D), bf16),
            pltpu.VMEM((TOK, D), bf16),
            pltpu.VMEM((9, 2, TOK, W), bf16),
            pltpu.VMEM((TOK, W), bf16),
            pltpu.VMEM((TOK, 2 * W), f32),
            pltpu.VMEM((TOK, W), f32),
            pltpu.VMEM((GROUP, W), bf16),
            pltpu.VMEM((8, ROWS, D), bf16),
            pltpu.VMEM((8, ROWS, D), bf16),
            pltpu.VMEM((8, ROWS, D), bf16),
            pltpu.VMEM((2, 2, HALF, D), bf16),
            pltpu.VMEM((2, 2, ROWS, D), bf16),
            pltpu.VMEM((ROWS, D), bf16),
            pltpu.SMEM((16,), jnp.int32),
            pltpu.SemaphoreType.DMA((8,)),
            pltpu.SemaphoreType.DMA((N_SEM,)),
            pltpu.SemaphoreType.DMA((N_SEM,)),
        ],
        compiler_params=pltpu.CompilerParams(
            collective_id=0, has_side_effects=True, vmem_limit_bytes=62 * 2**20
        ),
    )(*operands)


def solution(mesh):
    in_specs = (
        P("span", "seq", None),
        P("span", "seq", None),
        P("span", None, "seq"),
        P("span", None, "seq"),
        P(None, "seq"),
        P(None, "seq"),
        P(None, "seq"),
        P("seq", None),
        P(),
        P(),
        P(),
        P(),
        P(),
    )
    out_specs = P("span", "seq", None)
    return jax.shard_map(local, mesh=mesh, in_specs=in_specs, out_specs=out_specs, check_vma=False)
```

time: 451 us -> 144 us (0.32); the launches traced: 442 us -> 141 us
  waiting for transfers between devices: 248 us -> 0 us
  Pallas kernels: 0 us -> 138 us
  matrix products: 83.5 us -> 0 us
  other arithmetic: 48.3 us -> 0 us
  local copies, waits for them, and re-layouts: 42.9 us -> 3.31 us
  between operations: 19.6 us -> 0.01 us
    all_gather x3 -> x0, waiting for transfers between devices: 140 us -> none  [the longest x1 63 us: local(): lax.all_gather(normed, 'seq', axis=0, tiled=True)]
    pallas_call x0 -> x1, Pallas kernels: none -> 138 us  [local(): pl.pallas_call(kernel, out_shape=jax.ShapeDtypeStruct((1, ROWS, D), bf16)...]
    reduce_scatter x1 -> x0, waiting for transfers between devices: 107 us -> none  [local(): lax.psum_scatter(jnp.dot(attended, w_out, preferred_element_type=jnp.floa...]
    dot_general x20 -> x0, matrix products: 83.5 us -> none  [the longest x8 31.3 us: local(): jnp.einsum('hqk,khd->hqd', block_weights, vpart, preferred_element_type=j...]
    reduce_sum x15 -> x0, other arithmetic: 40.8 us -> none  [the longest x8 33.7 us: local(): jnp.sum(block_weights.astype(jnp.float32), axis=2)]
    slice x12 -> x0, local copies, waits for them, and re-layouts: 26.9 us -> none  [the longest x9 20.7 us: local(): value_rows = value_piece[offset]]
    unnamed x52 -> x2, local copies, waits for them, and re-layouts: 15.4 us -> 3.31 us
  transfers between devices with their start and end apart: 4 -> 0, of which waited for: 4 -> 0; matrix products, arithmetic and copies ran while one was open for 11% -> 0% of each run, Pallas kernels for 0% -> 0%
where the time goes in v1:
time: 144 us; the launch traced here: 141 us
  Pallas kernels  138 us (96%)
  local copies, waits for them, and re-layouts  3.31 us (2%)
    pallas_call x1, Pallas kernels, local(): pl.pallas_call(kernel, out_shape=jax.ShapeDtypeStruct((1, ROWS, D), bf16)...  138 us
    unnamed x2, local copies, waits for them, and re-layouts  3.31 us

profile of v1, /device:TPU:1, one launch (start us, length us, event | category | flops | bytes accessed | tf_op | source)
XLA Modules:
  0.0 141.2 jit_solution(534278275646074986)
XLA Ops:
  0.0 1.3 copy.14.plan
  1.3 137.8 %shard_map.127 = bf16[1,64,5120]{2,1,0:T(8,128)(2,1)} custom-call(bf16[1,64,5120]{2,1,0:T(8,128)(2,1)} %latent_hbm.1, bf16[1,64,5120]{2,1,0:T(8,128)(2,1)} %noise_hbm.1, bf16[1,1024,256]{2,1,0:T(8,128)(2,1)} %ck_hbm.1, bf16[1,1024,256]{2,1,0:T(8,128)(2,1)} %cv_hbm.1, bf16[5120,256]{1,0:T(8,128)(2,1)} %wq_hbm.1, bf16[5120,256]{1,0:T(8,128)(2,1)} %wk_hbm.1, ...), custom_call_target="tpu_custom_call" | custom-call | tf_op jit(solution)/shard_map/pallas_call | solution.py:410
  139.2 2.0 %copy.16 = bf16[1,64,5120]{2,1,0:T(8,128)(2,1)} copy(bf16[1,64,5120]{2,1,0:T(8,128)(2,1)} %shard_map.127) | data formatting | bytes 1310720

commit v2 on v1

--- a/solution.py
+++ b/solution.py
@@ -1,3 +1,5 @@
+import itertools
+
 import jax
 import jax.numpy as jnp
 from jax import lax
@@ -51,11 +53,10 @@
     acc,
     top,
     att,
-    p0,
-    p1,
     s,
     r1,
     r2,
+    xf,
     xb,
     flags,
     local_sem,
@@ -103,9 +104,10 @@
     pl.semaphore_wait(barrier, 7)
 
     started = []
+    count = itertools.count()
 
     def send(src, dst, device):
-        i = len(started)
+        i = next(count)
         copy = pltpu.make_async_remote_copy(
             src, dst, send_sem.at[i], recv_sem.at[i], device_id=device, device_id_type=MESH
         )
@@ -137,8 +139,8 @@
         return g.at[pl.ds(base + half * HALF, HALF)]
 
     step = step_index[span]
-    level_now = plan[step, 0]
-    level_next = plan[step, 1]
+    level_now = plan[0, step]
+    level_next = plan[1, step]
     loads["lat"].wait()
 
     @pl.loop(0, 4)
@@ -184,7 +186,8 @@
 
         @pl.loop(0, 3)
         def _(i):
-            y = jnp.dot(g[rows, :], w[i], preferred_element_type=jnp.float32).astype(jnp.bfloat16)
+            y = jnp.dot(g[rows, :], w[i], preferred_element_type=jnp.float32)
+            y = (y * jnp.where(i == 0, SCALE, 1.0)).astype(jnp.bfloat16)
 
             @pl.when(i == 0)
             def _():
@@ -196,35 +199,54 @@
 
     ones = jnp.ones((TOK, HD), jnp.bfloat16)
 
-    def attend(group, place):
-        rows = pl.ds(pl.multiple_of(group * GROUP, GROUP), GROUP)
-        seen = jnp.full((GROUP, HD), flags[place], jnp.int32) > 0
-        for h in range(W // HD):
+    def attend(groups, places):
+        items = [(pl.ds(pl.multiple_of(i * GROUP, GROUP), GROUP), h) for i in groups for h in range(W // HD)]
+        seen = [jnp.full((GROUP, HD), flags[place], jnp.int32) > 0 for place in places]
+        olds = [top[rows, h * HD : (h + 1) * HD] for rows, h in items]
+        scores, results = {}, {}
+
+        def score(i):
+            rows, h = items[i]
             cols = slice(h * HD, (h + 1) * HD)
-            scores = lax.dot_general(
-                q[rows, cols],
-                kv[place, 0, :, cols],
-                (((1,), (1,)), ((), ())),
-                preferred_element_type=jnp.float32,
+            scores[i] = [
+                lax.dot_general(
+                    q[rows, cols],
+                    kv[place, 0, :, cols],
+                    (((1,), (1,)), ((), ())),
+                    preferred_element_type=jnp.float32,
+                )
+                for place in places
+            ]
+
+        def weigh(i):
+            rows, h = items[i]
+            cols = slice(h * HD, (h + 1) * HD)
+            new = olds[i]
+            for mark, block in zip(seen, scores[i]):
+                new = jnp.where(mark, jnp.maximum(new, jnp.max(block, axis=1, keepdims=True)), new)
+            shrink = jnp.exp2(olds[i] - new)
+            lead = h * 2 * HD
+            value = acc[rows, lead : lead + HD] * shrink
+            total = acc[rows, lead + HD : lead + 2 * HD] * shrink
+            for mark, block, place in zip(seen, scores[i], places):
+                low = jnp.where(mark, new, HIGH)
+                weights = jnp.exp2(block - jnp.tile(low, (1, TOK // HD))).astype(jnp.bfloat16)
+                both = jnp.concatenate((kv[place, 1, :, cols], ones), axis=1)
+                sums = jnp.dot(weights, both, preferred_element_type=jnp.float32)
+                value = value + sums[:, :HD]
+                total = total + sums[:, HD:]
+            results[i] = (new, value, total)
+
+        score(0)
+        for i in range(len(items)):
+            if i + 1 < len(items):
+                score(i + 1)
+            weigh(i)
+        for i, (rows, h) in enumerate(items):
+            lead = h * 2 * HD
+            top[rows, h * HD : (h + 1) * HD], acc[rows, lead : lead + HD], acc[rows, lead + HD : lead + 2 * HD] = (
+                results[i]
             )
-            old = top[rows, cols]
-            peak = jnp.max(scores, axis=1, keepdims=True) * SCALE
-            new = jnp.where(seen, jnp.maximum(old, peak), old)
-            low = jnp.where(seen, new, HIGH)
-            weights = jnp.exp2(scores * SCALE - jnp.tile(low, (1, TOK // HD))).astype(jnp.bfloat16)
-            both = jnp.concatenate((kv[place, 1, :, cols], ones), axis=1)
-            sums = jnp.dot(weights, both, preferred_element_type=jnp.float32)
-            shrink = jnp.exp2(old - new)
-            wide = slice(h * 2 * HD, (h + 1) * 2 * HD)
-            acc[rows, wide] = acc[rows, wide] * jnp.tile(shrink, (1, 2)) + sums
-            top[rows, cols] = new
-
-    def attend_all(first_group, last_group, first_place, last_place):
-        groups = last_group - first_group + 1
-
-        @pl.loop(0, groups * (last_place - first_place + 1))
-        def _(i):
-            attend(first_group + i % groups, first_place + i // groups)
 
     for name in ("wq", "wk", "wv"):
         loads[name].wait()
@@ -246,26 +268,32 @@
         to_sibling((x, 3))
         to_sibling((x, 1))
 
+    y_fwd_up, y_fwd_down = {}, {}
+
+    def forward_y(x, j):
+        y_fwd_up[x, j] = send(part(CACHE[x, 3], 0, j), part(CACHE[x, 2], 0, j), yp)
+        y_fwd_down[x, j] = send(part(CACHE[x, 1], 1, j), part(CACHE[x, 2], 1, j), ym)
+
     forward_z(0)
     over[0, 1].wait_recv()
     over[0, 3].wait_recv()
     project(B)
-    attend_all(A, B, 0, 0)
+    attend([A, B], [0])
     for j in range(4):
         y_up[0, j].wait_recv()
         y_down[0, j].wait_recv()
-    attend_all(A, B, 1, 2)
+    x_over[0, 1].wait_recv()
+    y_up[1, 1] = send_piece((1, 0), (1, 3), 1, yp)
+    y_down[1, 1] = send_piece((1, 0), (1, 1), 1, ym)
+
+    @pl.loop(1, 3)
+    def _(place):
+        attend([A, B], [place])
+
     forward_z(1)
-    for j in (1, 2):
-        x_over[0, j].wait_recv()
-        y_up[1, j] = send_piece((1, 0), (1, 3), j, yp)
-        y_down[1, j] = send_piece((1, 0), (1, 1), j, ym)
-    y_fwd_up, y_fwd_down = {}, {}
-
-    def forward_y(x, j):
-        y_fwd_up[x, j] = send(part(CACHE[x, 3], 0, j), part(CACHE[x, 2], 0, j), yp)
-        y_fwd_down[x, j] = send(part(CACHE[x, 1], 1, j), part(CACHE[x, 2], 1, j), ym)
-
+    x_over[0, 2].wait_recv()
+    y_up[1, 2] = send_piece((1, 0), (1, 3), 2, yp)
+    y_down[1, 2] = send_piece((1, 0), (1, 1), 2, ym)
     for j in (3, 0, 1, 2):
         forward_y(0, j)
     for dy in (0, 1, 3):
@@ -273,28 +301,39 @@
     over[1, 1].wait_recv()
     over[1, 3].wait_recv()
     project(C)
-    attend_all(C, C, 0, 2)
-    for x in range(2):
-        z_fwd_up[x].wait_recv()
-        z_fwd_down[x].wait_recv()
-        to_sibling((x, 2))
+    attend([C], [0, 1])
+    z_fwd_up[0].wait_recv()
+    z_fwd_down[0].wait_recv()
+    to_sibling((0, 2))
     x_over[0, 3].wait_recv()
-    attend_all(A, C, 3, 3)
+    attend([A, B], [3])
     for j in range(3):
         y_up[1, j].wait_recv()
         y_down[1, j].wait_recv()
         forward_y(1, j)
+    z_fwd_up[1].wait_recv()
+    z_fwd_down[1].wait_recv()
+    to_sibling((1, 2))
     y_fwd_up[0, 3].wait_recv()
     y_fwd_down[0, 3].wait_recv()
     x_over[2, 3] = send_piece((0, 2), (1, 2), 3, xn)
+    attend([C], [2, 3])
     over[0, 2].wait_recv()
     over[1, 2].wait_recv()
     project(E)
-    attend_all(E, E, 0, 3)
-    attend_all(A, E, OWN, OWN)
+
+    @pl.loop(0, 2)
+    def _(i):
+        attend([E], [2 * i, 2 * i + 1])
+
+    attend([A, B, C, E], [OWN])
     x_over[1, 3].wait_recv()
     x_over[3, 3].wait_recv()
-    attend_all(A, E, 4, 5)
+
+    @pl.loop(4, 6)
+    def _(place):
+        attend([A, B, C, E], [place])
+
     for j in range(3):
         y_fwd_up[0, j].wait_recv()
         y_fwd_down[0, j].wait_recv()
@@ -305,10 +344,18 @@
     loads["wo"].wait()
     loads["noise"].wait()
 
+    for copy in started:
+        copy.wait_send()
+    started.clear()
+    p0 = g.at[pl.ds(0, 8 * ROWS)]
+    p1 = g.at[pl.ds(8 * ROWS, 8 * ROWS)]
     part_over = {}
 
+    def rows_at(place, first=0, count=ROWS):
+        return pl.ds(place * ROWS + first, count)
+
     def finish(group):
-        attend_all(group, group, 6, 7)
+        attend([group], [6, 7])
         rows = pl.ds(group * GROUP, GROUP)
         for h in range(W // HD):
             lead = h * 2 * HD
@@ -321,13 +368,13 @@
             cols = pl.ds(pl.multiple_of(i * 512, 512), 512)
             y = jnp.dot(att[...], wo[:, cols], preferred_element_type=jnp.float32)
             y = y.astype(jnp.bfloat16)
-            p0[2 * group, :, cols] = y[:ROWS]
-            p1[2 * group, :, cols] = y[ROWS : 2 * ROWS]
-            p0[2 * group + 1, :, cols] = y[2 * ROWS : 3 * ROWS]
-            p1[2 * group + 1, :, cols] = y[3 * ROWS :]
+            p0[rows_at(2 * group), cols] = y[:ROWS]
+            p1[rows_at(2 * group), cols] = y[ROWS : 2 * ROWS]
+            p0[rows_at(2 * group + 1), cols] = y[2 * ROWS : 3 * ROWS]
+            p1[rows_at(2 * group + 1), cols] = y[3 * ROWS :]
 
         for place in (2 * group + 1, 2 * group):
-            part_over[place] = send(p1.at[place], s.at[place], sib)
+            part_over[place] = send(p1.at[rows_at(place)], s.at[place], sib)
 
     def total(dst, *terms):
         count = dst.shape[0] // 16
@@ -340,69 +387,86 @@
                 value = value + term[rows, :].astype(jnp.float32)
             dst[rows, :] = value.astype(jnp.bfloat16)
 
-    half_rows = (pl.ds(0, HALF), pl.ds(HALF, HALF))
-    r1_up, r1_down, r2_up, r2_down = {}, {}, {}, {}
-
-    def first_hop(x):
-        place = PLACE[x, 2]
+    a, b = pl.ds(0, HALF), pl.ds(HALF, HALF)
+    quarter = HALF // 2
+    x_first, hop_up, hop_down, end_up, end_down = {}, {}, {}, {}, {}
+
+    def to_partner(z):
+        place = PLACE[1, z]
         part_over[place].wait_recv()
-        total(p0.at[place], p0.at[place], s.at[place])
-        r1_up[x] = send(p0.at[place, half_rows[0]], r1.at[x, 0], zp)
-        r1_down[x] = send(p0.at[place, half_rows[1]], r1.at[x, 1], zm)
-
-    def second_hop(x):
-        up, down = PLACE[x, 1], PLACE[x, 3]
-        part_over[up].wait_recv()
-        part_over[down].wait_recv()
-        a, b = half_rows
-        total(p0.at[up, b], p0.at[up, b], s.at[up, b])
-        r2_up[x, 1] = send(p0.at[up, b], r2.at[x, 0, b], zp)
-        total(p0.at[down, a], p0.at[down, a], s.at[down, a])
-        r2_down[x, 0] = send(p0.at[down, a], r2.at[x, 1, a], zm)
-        r1_up[x].wait_recv()
-        total(p0.at[up, a], p0.at[up, a], s.at[up, a], r1.at[x, 0])
-        r2_up[x, 0] = send(p0.at[up, a], r2.at[x, 0, a], zp)
-        r1_down[x].wait_recv()
-        total(p0.at[down, b], p0.at[down, b], s.at[down, b], r1.at[x, 1])
-        r2_down[x, 1] = send(p0.at[down, b], r2.at[x, 1, b], zm)
+        total(p0.at[rows_at(place, 0, HALF)], p0.at[rows_at(place, 0, HALF)], s.at[place, a])
+        x_first[z] = send(p0.at[rows_at(place, 0, HALF)], xf.at[z], x2)
+
+    def first_hop(way, place, rows, *terms):
+        total(p0.at[rows_at(place, rows.start, rows.size)], p0.at[rows_at(place, rows.start, rows.size)], s.at[place, rows], *terms)
+        hop_up[way] = send(p0.at[rows_at(place, rows.start, quarter)], r1.at[way, 0], zp)
+        hop_down[way] = send(p0.at[rows_at(place, rows.start + quarter, quarter)], r1.at[way, 1], zm)
+
+    def second_hop(way, up, down, rows, up_terms=(), down_terms=()):
+        total(p0.at[rows_at(up, rows.start, rows.size)], p0.at[rows_at(up, rows.start, rows.size)], s.at[up, rows], *up_terms)
+        total(p0.at[rows_at(down, rows.start, rows.size)], p0.at[rows_at(down, rows.start, rows.size)], s.at[down, rows], *down_terms)
+        low, high = pl.ds(rows.start, quarter), pl.ds(rows.start + quarter, quarter)
+        hop_up[way].wait_recv()
+        total(p0.at[rows_at(up, low.start, quarter)], p0.at[rows_at(up, low.start, quarter)], r1.at[way, 0])
+        end_up[way] = send(p0.at[rows_at(up, rows.start, rows.size)], r2.at[way, 0], zp)
+        hop_down[way].wait_recv()
+        total(p0.at[rows_at(down, high.start, quarter)], p0.at[rows_at(down, high.start, quarter)], r1.at[way, 1])
+        end_down[way] = send(p0.at[rows_at(down, rows.start, rows.size)], r2.at[way, 1], zm)
 
     finish(E)
     finish(C)
-    first_hop(1)
-    first_hop(0)
+    to_partner(2)
+    first_hop(1, PLACE[1, 2], b)
+    part_over[PLACE[0, 2]].wait_recv()
+    first_hop(0, PLACE[0, 2], b)
     finish(B)
+    to_partner(1)
+    to_partner(3)
+    second_hop(1, PLACE[1, 1], PLACE[1, 3], b)
     finish(A)
-    second_hop(1)
-    second_hop(0)
-    part_over[1].wait_recv()
-    last = {}
-    for h, rows in ((0, half_rows[0]), (1, half_rows[1])):
-        r2_up[1, h].wait_recv()
-        r2_down[1, h].wait_recv()
-        total(p0.at[1, rows], p0.at[1, rows], s.at[1, rows], r2.at[1, 0, rows], r2.at[1, 1, rows])
-        last[h] = send(p0.at[1, rows], xb.at[rows], x2)
+    to_partner(0)
+    part_over[PLACE[0, 1]].wait_recv()
+    part_over[PLACE[0, 3]].wait_recv()
+    second_hop(0, PLACE[0, 1], PLACE[0, 3], b)
+    x_first[2].wait_recv()
+    first_hop(2, PLACE[0, 2], a, xf.at[2])
+    end_up[1].wait_recv()
+    end_down[1].wait_recv()
+    total(p0.at[rows_at(1, HALF, HALF)], p0.at[rows_at(1, HALF, HALF)], s.at[1, b], r2.at[1, 0], r2.at[1, 1])
+    last = send(p0.at[rows_at(1, HALF, HALF)], xb, x2)
+    x_first[1].wait_recv()
+    x_first[3].wait_recv()
+    second_hop(2, PLACE[0, 1], PLACE[0, 3], a, (xf.at[1],), (xf.at[3],))
     part_over[0].wait_recv()
-    for h in range(2):
-        r2_up[0, h].wait_recv()
-        r2_down[0, h].wait_recv()
-        last[h].wait_recv()
-
-    @pl.loop(0, 4)
-    def _(i):
-        rows = pl.ds(pl.multiple_of(i * 16, 16), 16)
-        mixed = p0[0, rows, :].astype(jnp.float32) + s[0, rows, :].astype(jnp.float32)
-        mixed = mixed + r2[0, 0, rows, :].astype(jnp.float32) + r2[0, 1, rows, :].astype(jnp.float32)
-        mixed = mixed + xb[rows, :].astype(jnp.float32)
-        xrows = lat[rows, :].astype(jnp.float32)
-        fresh = noise[rows, :].astype(jnp.float32)
-        result = (1.0 - level_next) * (xrows - level_now * (xrows + mixed)) + level_next * fresh
-        out[0, rows, :] = result.astype(jnp.bfloat16)
+
+    def renoise(way, first, partner):
+        @pl.loop(0, HALF // 16)
+        def _(i):
+            rows = pl.ds(pl.multiple_of(first + i * 16, 16), 16)
+            here = pl.ds(pl.multiple_of(i * 16, 16), 16)
+            mixed = p0[rows, :].astype(jnp.float32) + s[0, rows, :].astype(jnp.float32)
+            mixed = mixed + r2[way, 0, here, :].astype(jnp.float32) + r2[way, 1, here, :].astype(jnp.float32)
+            mixed = mixed + partner[here, :].astype(jnp.float32)
+            xrows = lat[rows, :].astype(jnp.float32)
+            fresh = noise[rows, :].astype(jnp.float32)
+            result = (1.0 - level_next) * (xrows - level_now * (xrows + mixed)) + level_next * fresh
+            out[0, rows, :] = result.astype(jnp.bfloat16)
+
+    end_up[0].wait_recv()
+    end_down[0].wait_recv()
+    last.wait_recv()
+    renoise(0, HALF, xb)
+    x_first[0].wait_recv()
+    end_up[2].wait_recv()
+    end_down[2].wait_recv()
+    renoise(2, 0, xf.at[0])
 
     for copy in started:
         copy.wait_send()
 
 
 def local(*operands):
+    operands = operands[:9] + (operands[9].T,) + operands[10:]
     bf16, f32 = jnp.bfloat16, jnp.float32
     anywhere = pl.BlockSpec(memory_space=pl.ANY)
     vmem = pl.BlockSpec(memory_space=pltpu.VMEM)
@@ -424,11 +488,10 @@
             pltpu.VMEM((TOK, W), f32),
             pltpu.VMEM((GROUP, W), bf16),
             pltpu.VMEM((8, ROWS, D), bf16),
-            pltpu.VMEM((8, ROWS, D), bf16),
-            pltpu.VMEM((8, ROWS, D), bf16),
-            pltpu.VMEM((2, 2, HALF, D), bf16),
-            pltpu.VMEM((2, 2, ROWS, D), bf16),
-            pltpu.VMEM((ROWS, D), bf16),
+            pltpu.VMEM((3, 2, HALF // 2, D), bf16),
+            pltpu.VMEM((3, 2, HALF, D), bf16),
+            pltpu.VMEM((4, HALF, D), bf16),
+            pltpu.VMEM((HALF, D), bf16),
             pltpu.SMEM((16,), jnp.int32),
             pltpu.SemaphoreType.DMA((8,)),
             pltpu.SemaphoreType.DMA((N_SEM,)),

time: 144 us -> 123 us (0.85); the launches traced: 141 us -> 122 us
  Pallas kernels: 138 us -> 120 us
    pallas_call x1, Pallas kernels: 138 us -> 120 us  [local(): pl.pallas_call(kernel, out_shape=jax.ShapeDtypeStruct((1, ROWS, D), bf16)...]
    unnamed x2 -> x1, local copies, waits for them, and re-layouts: 3.31 us -> 1.97 us
where the time goes in v2:
time: 123 us; the launch traced here: 122 us
  Pallas kernels  120 us (98%)
  local copies, waits for them, and re-layouts  1.97 us (2%)
    pallas_call x1, Pallas kernels, local(): pl.pallas_call(kernel, out_shape=jax.ShapeDtypeStruct((1, ROWS, D), bf16)...  120 us

profile of v2, /device:TPU:1, one launch (start us, length us, event | category | flops | bytes accessed | tf_op | source)
XLA Modules:
  0.0 122.1 jit_solution(18203657512748730174)
XLA Ops:
  0.0 120.2 %shard_map.127 = bf16[1,64,5120]{2,1,0:T(8,128)(2,1)} custom-call(bf16[1,64,5120]{2,1,0:T(8,128)(2,1)} %latent_hbm.1, bf16[1,64,5120]{2,1,0:T(8,128)(2,1)} %noise_hbm.1, bf16[1,1024,256]{2,1,0:T(8,128)(2,1)} %ck_hbm.1, bf16[1,1024,256]{2,1,0:T(8,128)(2,1)} %cv_hbm.1, bf16[5120,256]{1,0:T(8,128)(2,1)} %wq_hbm.1, bf16[5120,256]{1,0:T(8,128)(2,1)} %wk_hbm.1, ...), custom_call_target="tpu_custom_call" | custom-call | tf_op jit(solution)/shard_map/pallas_call | solution.py:474
  120.2 2.0 %copy.15 = bf16[1,64,5120]{2,1,0:T(8,128)(2,1)} copy(bf16[1,64,5120]{2,1,0:T(8,128)(2,1)} %shard_map.127) | data formatting | bytes 1310720

commit v3 on v2

--- a/solution.py
+++ b/solution.py
@@ -14,7 +14,8 @@
 ROWS = 64
 HALF = 32
 GROUP = 256
-PIECE = 256
+PIECES = ((0, 240), (240, 240), (480, 224), (704, 320))
+X_COLS = 2304
 LOG2E = 1.4426950408889634
 SCALE = LOG2E / HD**0.5
 LOW = -1e30
@@ -25,7 +26,8 @@
 PLACE = {(0, 0): 0, (1, 0): 1, (0, 1): 2, (0, 3): 3, (1, 1): 4, (1, 3): 5, (0, 2): 6, (1, 2): 7}
 CACHE = {(0, 0): 0, (0, 1): 1, (0, 3): 2, (1, 0): 3, (1, 1): 4, (1, 3): 5, (0, 2): 6, (1, 2): 7}
 OWN = 8
-A, B, C, E = 0, 1, 2, 3
+A, B, C, E = (0, 256), (256, 256), (512, 256), (768, 256)
+E_LEFT, E_RIGHT = (768, 128), (896, 128)
 
 
 def kernel(
@@ -54,8 +56,10 @@
     top,
     att,
     s,
-    r1,
-    r2,
+    r1_a,
+    r1_b,
+    r2_a,
+    r2_b,
     xf,
     xb,
     flags,
@@ -101,8 +105,6 @@
     barrier = pltpu.get_barrier_semaphore()
     for device in (sib, x2, zp, zm, xn, yp, ym):
         pl.semaphore_signal(barrier, 1, device_id=device, device_id_type=MESH)
-    pl.semaphore_wait(barrier, 7)
-
     started = []
     count = itertools.count()
 
@@ -116,21 +118,13 @@
         return copy
 
     def piece(place, j):
-        return kv.at[place, :, pl.ds(j * PIECE, PIECE)]
+        return kv.at[place, :, pl.ds(*PIECES[j])]
 
     def part(place, side, j):
-        return kv.at[place, side, pl.ds(j * PIECE, PIECE)]
+        return kv.at[place, side, pl.ds(*PIECES[j])]
 
     def send_piece(src, dst, j, device):
         return send(piece(CACHE[src], j), piece(CACHE[dst], j), device)
-
-    loads["k"].wait()
-    loads["v"].wait()
-    y_up, y_down, x_over = {}, {}, {}
-    for j in range(4):
-        y_up[0, j] = send_piece((0, 0), (0, 3), j, yp)
-        y_down[0, j] = send_piece((0, 0), (0, 1), j, ym)
-    x_over[0, 0] = send_piece((0, 0), (1, 0), 0, xn)
 
     def rows_of(place, sub, half=None):
         base = PLACE[place] * 2 * ROWS + sub * ROWS
@@ -152,6 +146,16 @@
         scale = modulation[step, 1:2, :]
         g[rows, :] = (values * rms * (1.0 + scale) + shift).astype(jnp.bfloat16)
 
+    mine = assignment[span]
+    for (dx, dy), place in CACHE.items():
+        other = ((x_lo + dx) % 2) * 4 + (y + dy) % 4
+        flags[place] = visible[mine, assignment[other]]
+    flags[OWN] = 1
+
+    acc[...] = jnp.zeros_like(acc)
+    top[...] = jnp.full_like(top, LOW)
+
+    pl.semaphore_wait(barrier, 7)
     x_part, z_up, z_down, over = {}, {}, {}, {}
     for h in range(2):
         x_part[h] = send(rows_of((0, 0), 0, h), rows_of((1, 0), 0, h), x2)
@@ -164,25 +168,22 @@
 
     to_sibling((0, 0))
 
-    mine = assignment[span]
-    for (dx, dy), place in CACHE.items():
-        other = ((x_lo + dx) % 2) * 4 + (y + dy) % 4
-        flags[place] = visible[mine, assignment[other]]
-    flags[OWN] = 1
-
-    acc[...] = jnp.zeros_like(acc)
-    top[...] = jnp.full_like(top, LOW)
+    loads["k"].wait()
+    loads["v"].wait()
+    y_up, y_down, x_over = {}, {}, {}
+    for j in range(4):
+        y_up[0, j] = send_piece((0, 0), (0, 3), j, yp)
+        y_down[0, j] = send_piece((0, 0), (0, 1), j, ym)
+    for j in range(3):
+        x_over[0, j] = send_piece((0, 0), (1, 0), j, xn)
 
     for h in range(2):
         x_part[h].wait_recv()
         z_up[1, h] = send(rows_of((1, 0), 0, h), rows_of((1, 3), 0, h), zp)
         z_down[1, h] = send(rows_of((1, 0), 0, h), rows_of((1, 1), 0, h), zm)
     to_sibling((1, 0))
-    for j in (1, 2):
-        x_over[0, j] = send_piece((0, 0), (1, 0), j, xn)
-
     def project(group):
-        rows = pl.ds(group * GROUP, GROUP)
+        rows = pl.ds(*group)
 
         @pl.loop(0, 3)
         def _(i):
@@ -200,8 +201,9 @@
     ones = jnp.ones((TOK, HD), jnp.bfloat16)
 
     def attend(groups, places):
-        items = [(pl.ds(pl.multiple_of(i * GROUP, GROUP), GROUP), h) for i in groups for h in range(W // HD)]
-        seen = [jnp.full((GROUP, HD), flags[place], jnp.int32) > 0 for place in places]
+        items = [(pl.ds(*group), h) for group in groups for h in range(W // HD)]
+        seen = [jnp.full((8, HD), flags[place], jnp.int32) > 0 for place in places]
+        seen = [{count: jnp.tile(mark, (count // 8, 1)) for _, count in groups} for mark in seen]
         olds = [top[rows, h * HD : (h + 1) * HD] for rows, h in items]
         scores, results = {}, {}
 
@@ -222,13 +224,14 @@
             rows, h = items[i]
             cols = slice(h * HD, (h + 1) * HD)
             new = olds[i]
-            for mark, block in zip(seen, scores[i]):
+            marks = [mark[rows.size] for mark in seen]
+            for mark, block in zip(marks, scores[i]):
                 new = jnp.where(mark, jnp.maximum(new, jnp.max(block, axis=1, keepdims=True)), new)
             shrink = jnp.exp2(olds[i] - new)
             lead = h * 2 * HD
             value = acc[rows, lead : lead + HD] * shrink
             total = acc[rows, lead + HD : lead + 2 * HD] * shrink
-            for mark, block, place in zip(seen, scores[i], places):
+            for mark, block, place in zip(marks, scores[i], places):
                 low = jnp.where(mark, new, HIGH)
                 weights = jnp.exp2(block - jnp.tile(low, (1, TOK // HD))).astype(jnp.bfloat16)
                 both = jnp.concatenate((kv[place, 1, :, cols], ones), axis=1)
@@ -248,15 +251,6 @@
                 results[i]
             )
 
-    for name in ("wq", "wk", "wv"):
-        loads[name].wait()
-    x_over[0, 0].wait_recv()
-    y_up[1, 0] = send_piece((1, 0), (1, 3), 0, yp)
-    y_down[1, 0] = send_piece((1, 0), (1, 1), 0, ym)
-    over[0, 0].wait_recv()
-    over[1, 0].wait_recv()
-    project(A)
-
     z_fwd_up, z_fwd_down = {}, {}
 
     def forward_z(x):
@@ -274,7 +268,18 @@
         y_fwd_up[x, j] = send(part(CACHE[x, 3], 0, j), part(CACHE[x, 2], 0, j), yp)
         y_fwd_down[x, j] = send(part(CACHE[x, 1], 1, j), part(CACHE[x, 2], 1, j), ym)
 
+    def forward_x(j):
+        x_over[0, j].wait_recv()
+        y_up[1, j] = send_piece((1, 0), (1, 3), j, yp)
+        y_down[1, j] = send_piece((1, 0), (1, 1), j, ym)
+
     forward_z(0)
+    for name in ("wq", "wk", "wv"):
+        loads[name].wait()
+    over[0, 0].wait_recv()
+    over[1, 0].wait_recv()
+    project(A)
+    forward_x(0)
     over[0, 1].wait_recv()
     over[0, 3].wait_recv()
     project(B)
@@ -282,22 +287,18 @@
     for j in range(4):
         y_up[0, j].wait_recv()
         y_down[0, j].wait_recv()
-    x_over[0, 1].wait_recv()
-    y_up[1, 1] = send_piece((1, 0), (1, 3), 1, yp)
-    y_down[1, 1] = send_piece((1, 0), (1, 1), 1, ym)
+    forward_x(1)
+    for dy in (0, 1, 3):
+        x_over[dy, 3] = send_piece((0, dy), (1, dy), 3, xn)
 
     @pl.loop(1, 3)
     def _(place):
         attend([A, B], [place])
 
-    forward_z(1)
-    x_over[0, 2].wait_recv()
-    y_up[1, 2] = send_piece((1, 0), (1, 3), 2, yp)
-    y_down[1, 2] = send_piece((1, 0), (1, 1), 2, ym)
+    forward_x(2)
     for j in (3, 0, 1, 2):
         forward_y(0, j)
-    for dy in (0, 1, 3):
-        x_over[dy, 3] = send_piece((0, dy), (1, dy), 3, xn)
+    forward_z(1)
     over[1, 1].wait_recv()
     over[1, 3].wait_recv()
     project(C)
@@ -307,36 +308,35 @@
     to_sibling((0, 2))
     x_over[0, 3].wait_recv()
     attend([A, B], [3])
+    attend([C], [2, 3])
+    over[0, 2].wait_recv()
+    project(E_LEFT)
     for j in range(3):
         y_up[1, j].wait_recv()
         y_down[1, j].wait_recv()
         forward_y(1, j)
+    y_fwd_up[0, 3].wait_recv()
+    y_fwd_down[0, 3].wait_recv()
+    x_over[2, 3] = send_piece((0, 2), (1, 2), 3, xn)
     z_fwd_up[1].wait_recv()
     z_fwd_down[1].wait_recv()
     to_sibling((1, 2))
-    y_fwd_up[0, 3].wait_recv()
-    y_fwd_down[0, 3].wait_recv()
-    x_over[2, 3] = send_piece((0, 2), (1, 2), 3, xn)
-    attend([C], [2, 3])
-    over[0, 2].wait_recv()
+    attend([E_LEFT], [0, 1, 2, 3])
+    x_over[1, 3].wait_recv()
+    attend([A, B, C, E_LEFT], [4])
     over[1, 2].wait_recv()
-    project(E)
-
-    @pl.loop(0, 2)
-    def _(i):
-        attend([E], [2 * i, 2 * i + 1])
-
+    project(E_RIGHT)
+    attend([E_RIGHT], [0, 1, 2, 3, 4])
     attend([A, B, C, E], [OWN])
-    x_over[1, 3].wait_recv()
     x_over[3, 3].wait_recv()
-
-    @pl.loop(4, 6)
-    def _(place):
-        attend([A, B, C, E], [place])
-
     for j in range(3):
         y_fwd_up[0, j].wait_recv()
         y_fwd_down[0, j].wait_recv()
+
+    @pl.loop(5, 7)
+    def _(place):
+        attend([A, B, C, E], [place])
+
     for j in range(3):
         y_fwd_up[1, j].wait_recv()
         y_fwd_down[1, j].wait_recv()
@@ -355,25 +355,27 @@
         return pl.ds(place * ROWS + first, count)
 
     def finish(group):
-        attend([group], [6, 7])
-        rows = pl.ds(group * GROUP, GROUP)
+        attend([group], [7])
+        rows = pl.ds(*group)
         for h in range(W // HD):
             lead = h * 2 * HD
             att[:, h * HD : (h + 1) * HD] = (
                 acc[rows, lead : lead + HD] / acc[rows, lead + HD : lead + 2 * HD]
             ).astype(jnp.bfloat16)
-
-        @pl.loop(0, 10)
+        first = group[0] // (2 * ROWS)
+
+        @pl.loop(0, 2)
         def _(i):
-            cols = pl.ds(pl.multiple_of(i * 512, 512), 512)
-            y = jnp.dot(att[...], wo[:, cols], preferred_element_type=jnp.float32)
-            y = y.astype(jnp.bfloat16)
-            p0[rows_at(2 * group), cols] = y[:ROWS]
-            p1[rows_at(2 * group), cols] = y[ROWS : 2 * ROWS]
-            p0[rows_at(2 * group + 1), cols] = y[2 * ROWS : 3 * ROWS]
-            p1[rows_at(2 * group + 1), cols] = y[3 * ROWS :]
-
-        for place in (2 * group + 1, 2 * group):
+            for k in range(5):
+                cols = pl.ds(pl.multiple_of(i * (D // 2) + k * 512, 512), 512)
+                y = jnp.dot(att[...], wo[:, cols], preferred_element_type=jnp.float32)
+                y = y.astype(jnp.bfloat16)
+                p0[rows_at(first), cols] = y[:ROWS]
+                p1[rows_at(first), cols] = y[ROWS : 2 * ROWS]
+                p0[rows_at(first + 1), cols] = y[2 * ROWS : 3 * ROWS]
+                p1[rows_at(first + 1), cols] = y[3 * ROWS :]
+
+        for place in (first + 1, first):
             part_over[place] = send(p1.at[rows_at(place)], s.at[place], sib)
 
     def total(dst, *terms):
@@ -387,79 +389,80 @@
                 value = value + term[rows, :].astype(jnp.float32)
             dst[rows, :] = value.astype(jnp.bfloat16)
 
-    a, b = pl.ds(0, HALF), pl.ds(HALF, HALF)
-    quarter = HALF // 2
+    a, b = pl.ds(0, X_COLS), pl.ds(X_COLS, D - X_COLS)
     x_first, hop_up, hop_down, end_up, end_down = {}, {}, {}, {}, {}
+
+    def sum_at(place, cols, *terms, first=0, count=ROWS):
+        dst = p0.at[rows_at(place, first, count), cols]
+        total(dst, dst, *terms)
 
     def to_partner(z):
         place = PLACE[1, z]
         part_over[place].wait_recv()
-        total(p0.at[rows_at(place, 0, HALF)], p0.at[rows_at(place, 0, HALF)], s.at[place, a])
-        x_first[z] = send(p0.at[rows_at(place, 0, HALF)], xf.at[z], x2)
-
-    def first_hop(way, place, rows, *terms):
-        total(p0.at[rows_at(place, rows.start, rows.size)], p0.at[rows_at(place, rows.start, rows.size)], s.at[place, rows], *terms)
-        hop_up[way] = send(p0.at[rows_at(place, rows.start, quarter)], r1.at[way, 0], zp)
-        hop_down[way] = send(p0.at[rows_at(place, rows.start + quarter, quarter)], r1.at[way, 1], zm)
-
-    def second_hop(way, up, down, rows, up_terms=(), down_terms=()):
-        total(p0.at[rows_at(up, rows.start, rows.size)], p0.at[rows_at(up, rows.start, rows.size)], s.at[up, rows], *up_terms)
-        total(p0.at[rows_at(down, rows.start, rows.size)], p0.at[rows_at(down, rows.start, rows.size)], s.at[down, rows], *down_terms)
-        low, high = pl.ds(rows.start, quarter), pl.ds(rows.start + quarter, quarter)
+        sum_at(place, a, s.at[place, :, a])
+        x_first[z] = send(p0.at[rows_at(place), a], xf.at[z], x2)
+
+    def first_hop(way, place, cols, r1, *terms):
+        sum_at(place, cols, s.at[place, :, cols], *terms)
+        hop_up[way] = send(p0.at[rows_at(place, 0, HALF), cols], r1.at[0], zp)
+        hop_down[way] = send(p0.at[rows_at(place, HALF, HALF), cols], r1.at[1], zm)
+
+    def second_hop(way, up, down, cols, r1, r2, up_terms=(), down_terms=()):
+        sum_at(up, cols, s.at[up, :, cols], *up_terms)
+        sum_at(down, cols, s.at[down, :, cols], *down_terms)
         hop_up[way].wait_recv()
-        total(p0.at[rows_at(up, low.start, quarter)], p0.at[rows_at(up, low.start, quarter)], r1.at[way, 0])
-        end_up[way] = send(p0.at[rows_at(up, rows.start, rows.size)], r2.at[way, 0], zp)
+        sum_at(up, cols, r1.at[0], count=HALF)
+        end_up[way] = send(p0.at[rows_at(up), cols], r2.at[0], zp)
         hop_down[way].wait_recv()
-        total(p0.at[rows_at(down, high.start, quarter)], p0.at[rows_at(down, high.start, quarter)], r1.at[way, 1])
-        end_down[way] = send(p0.at[rows_at(down, rows.start, rows.size)], r2.at[way, 1], zm)
+        sum_at(down, cols, r1.at[1], first=HALF, count=HALF)
+        end_down[way] = send(p0.at[rows_at(down), cols], r2.at[1], zm)
 
     finish(E)
     finish(C)
     to_partner(2)
-    first_hop(1, PLACE[1, 2], b)
+    first_hop(1, PLACE[1, 2], b, r1_b.at[1])
     part_over[PLACE[0, 2]].wait_recv()
-    first_hop(0, PLACE[0, 2], b)
+    first_hop(0, PLACE[0, 2], b, r1_b.at[0])
     finish(B)
     to_partner(1)
     to_partner(3)
-    second_hop(1, PLACE[1, 1], PLACE[1, 3], b)
+    second_hop(1, PLACE[1, 1], PLACE[1, 3], b, r1_b.at[1], r2_b.at[1])
     finish(A)
     to_partner(0)
     part_over[PLACE[0, 1]].wait_recv()
     part_over[PLACE[0, 3]].wait_recv()
-    second_hop(0, PLACE[0, 1], PLACE[0, 3], b)
+    second_hop(0, PLACE[0, 1], PLACE[0, 3], b, r1_b.at[0], r2_b.at[0])
     x_first[2].wait_recv()
-    first_hop(2, PLACE[0, 2], a, xf.at[2])
+    first_hop(2, PLACE[0, 2], a, r1_a, xf.at[2])
     end_up[1].wait_recv()
     end_down[1].wait_recv()
-    total(p0.at[rows_at(1, HALF, HALF)], p0.at[rows_at(1, HALF, HALF)], s.at[1, b], r2.at[1, 0], r2.at[1, 1])
-    last = send(p0.at[rows_at(1, HALF, HALF)], xb, x2)
+    sum_at(1, b, s.at[1, :, b], r2_b.at[1, 0], r2_b.at[1, 1])
+    last = send(p0.at[rows_at(1), b], xb, x2)
     x_first[1].wait_recv()
     x_first[3].wait_recv()
-    second_hop(2, PLACE[0, 1], PLACE[0, 3], a, (xf.at[1],), (xf.at[3],))
+    second_hop(2, PLACE[0, 1], PLACE[0, 3], a, r1_a, r2_a, (xf.at[1],), (xf.at[3],))
     part_over[0].wait_recv()
 
-    def renoise(way, first, partner):
-        @pl.loop(0, HALF // 16)
+    def renoise(cols, r2, partner):
+        @pl.loop(0, ROWS // 16)
         def _(i):
-            rows = pl.ds(pl.multiple_of(first + i * 16, 16), 16)
-            here = pl.ds(pl.multiple_of(i * 16, 16), 16)
-            mixed = p0[rows, :].astype(jnp.float32) + s[0, rows, :].astype(jnp.float32)
-            mixed = mixed + r2[way, 0, here, :].astype(jnp.float32) + r2[way, 1, here, :].astype(jnp.float32)
-            mixed = mixed + partner[here, :].astype(jnp.float32)
-            xrows = lat[rows, :].astype(jnp.float32)
-            fresh = noise[rows, :].astype(jnp.float32)
+            rows = pl.ds(pl.multiple_of(i * 16, 16), 16)
+            mixed = p0[rows, cols].astype(jnp.float32) + s[0, rows, cols].astype(jnp.float32)
+            mixed = mixed + r2[0, rows, :].astype(jnp.float32) + r2[1, rows, :].astype(jnp.float32)
+            mixed = mixed + partner[rows, :].astype(jnp.float32)
+            xrows = lat[rows, cols].astype(jnp.float32)
+            fresh = noise[rows, cols].astype(jnp.float32)
             result = (1.0 - level_next) * (xrows - level_now * (xrows + mixed)) + level_next * fresh
-            out[0, rows, :] = result.astype(jnp.bfloat16)
+            out[0, rows, cols] = result.astype(jnp.bfloat16)
 
     end_up[0].wait_recv()
     end_down[0].wait_recv()
     last.wait_recv()
-    renoise(0, HALF, xb)
+    renoise(b, r2_b.at[0], xb)
     x_first[0].wait_recv()
     end_up[2].wait_recv()
     end_down[2].wait_recv()
-    renoise(2, 0, xf.at[0])
+    renoise(a, r2_a, xf.at[0])
 
     for copy in started:
         copy.wait_send()
@@ -488,10 +491,12 @@
             pltpu.VMEM((TOK, W), f32),
             pltpu.VMEM((GROUP, W), bf16),
             pltpu.VMEM((8, ROWS, D), bf16),
-            pltpu.VMEM((3, 2, HALF // 2, D), bf16),
-            pltpu.VMEM((3, 2, HALF, D), bf16),
-            pltpu.VMEM((4, HALF, D), bf16),
-            pltpu.VMEM((HALF, D), bf16),
+            pltpu.VMEM((2, HALF, X_COLS), bf16),
+            pltpu.VMEM((2, 2, HALF, D - X_COLS), bf16),
+            pltpu.VMEM((2, ROWS, X_COLS), bf16),
+            pltpu.VMEM((2, 2, ROWS, D - X_COLS), bf16),
+            pltpu.VMEM((4, ROWS, X_COLS), bf16),
+            pltpu.VMEM((ROWS, D - X_COLS), bf16),
             pltpu.SMEM((16,), jnp.int32),
             pltpu.SemaphoreType.DMA((8,)),
             pltpu.SemaphoreType.DMA((N_SEM,)),

time: 123 us -> 115 us (0.935)
  Pallas kernels: 120 us -> 113 us
    pallas_call x1, Pallas kernels: 120 us -> 113 us  [local(): pl.pallas_call(kernel, out_shape=jax.ShapeDtypeStruct((1, ROWS, D), bf16)...]
where the time goes in v3:
time: 115 us
  Pallas kernels  113 us (98%)
  local copies, waits for them, and re-layouts  1.97 us (2%)
    pallas_call x1, Pallas kernels, local(): pl.pallas_call(kernel, out_shape=jax.ShapeDtypeStruct((1, ROWS, D), bf16)...  113 us

profile of v3, /device:TPU:1, one launch (start us, length us, event | category | flops | bytes accessed | tf_op | source)
XLA Modules:
  0.0 115.2 jit_solution(4600039789864955414)
XLA Ops:
  0.0 113.2 %shard_map.127 = bf16[1,64,5120]{2,1,0:T(8,128)(2,1)} custom-call(bf16[1,64,5120]{2,1,0:T(8,128)(2,1)} %latent_hbm.1, bf16[1,64,5120]{2,1,0:T(8,128)(2,1)} %noise_hbm.1, bf16[1,1024,256]{2,1,0:T(8,128)(2,1)} %ck_hbm.1, bf16[1,1024,256]{2,1,0:T(8,128)(2,1)} %cv_hbm.1, bf16[5120,256]{1,0:T(8,128)(2,1)} %wq_hbm.1, bf16[5120,256]{1,0:T(8,128)(2,1)} %wk_hbm.1, ...), custom_call_target="tpu_custom_call" | custom-call | tf_op jit(solution)/shard_map/pallas_call | solution.py:477
  113.2 2.0 %copy.15 = bf16[1,64,5120]{2,1,0:T(8,128)(2,1)} copy(bf16[1,64,5120]{2,1,0:T(8,128)(2,1)} %shard_map.127) | data formatting | bytes 1310720

commit v4 on v3

--- a/solution.py
+++ b/solution.py
@@ -13,7 +13,6 @@
 W = 256
 ROWS = 64
 HALF = 32
-GROUP = 256
 PIECES = ((0, 240), (240, 240), (480, 224), (704, 320))
 X_COLS = 2304
 LOG2E = 1.4426950408889634
@@ -333,10 +332,7 @@
         y_fwd_up[0, j].wait_recv()
         y_fwd_down[0, j].wait_recv()
 
-    @pl.loop(5, 7)
-    def _(place):
-        attend([A, B, C, E], [place])
-
+    attend([E], [5, 6])
     for j in range(3):
         y_fwd_up[1, j].wait_recv()
         y_fwd_down[1, j].wait_recv()
@@ -354,28 +350,29 @@
     def rows_at(place, first=0, count=ROWS):
         return pl.ds(place * ROWS + first, count)
 
-    def finish(group):
-        attend([group], [7])
-        rows = pl.ds(*group)
+    def finish(group, places):
+        attend([group], places)
+        start, count = group
+        rows, here = pl.ds(start, count), pl.ds(0, count)
         for h in range(W // HD):
             lead = h * 2 * HD
-            att[:, h * HD : (h + 1) * HD] = (
+            att[here, h * HD : (h + 1) * HD] = (
                 acc[rows, lead : lead + HD] / acc[rows, lead + HD : lead + 2 * HD]
             ).astype(jnp.bfloat16)
-        first = group[0] // (2 * ROWS)
+        blocks = range(start // (2 * ROWS), (start + count) // (2 * ROWS))
 
         @pl.loop(0, 2)
         def _(i):
             for k in range(5):
                 cols = pl.ds(pl.multiple_of(i * (D // 2) + k * 512, 512), 512)
-                y = jnp.dot(att[...], wo[:, cols], preferred_element_type=jnp.float32)
+                y = jnp.dot(att[here, :], wo[:, cols], preferred_element_type=jnp.float32)
                 y = y.astype(jnp.bfloat16)
-                p0[rows_at(first), cols] = y[:ROWS]
-                p1[rows_at(first), cols] = y[ROWS : 2 * ROWS]
-                p0[rows_at(first + 1), cols] = y[2 * ROWS : 3 * ROWS]
-                p1[rows_at(first + 1), cols] = y[3 * ROWS :]
-
-        for place in (first + 1, first):
+                for n, place in enumerate(blocks):
+                    lead = n * 2 * ROWS
+                    p0[rows_at(place), cols] = y[lead : lead + ROWS]
+                    p1[rows_at(place), cols] = y[lead + ROWS : lead + 2 * ROWS]
+
+        for place in blocks:
             part_over[place] = send(p1.at[rows_at(place)], s.at[place], sib)
 
     def total(dst, *terms):
@@ -417,17 +414,18 @@
         sum_at(down, cols, r1.at[1], first=HALF, count=HALF)
         end_down[way] = send(p0.at[rows_at(down), cols], r2.at[1], zm)
 
-    finish(E)
-    finish(C)
+    finish(E_RIGHT, [7])
+    finish(E_LEFT, [7])
     to_partner(2)
     first_hop(1, PLACE[1, 2], b, r1_b.at[1])
+    finish(C, [5, 6, 7])
     part_over[PLACE[0, 2]].wait_recv()
     first_hop(0, PLACE[0, 2], b, r1_b.at[0])
-    finish(B)
+    finish(B, [5, 6, 7])
     to_partner(1)
     to_partner(3)
     second_hop(1, PLACE[1, 1], PLACE[1, 3], b, r1_b.at[1], r2_b.at[1])
-    finish(A)
+    finish(A, [5, 6, 7])
     to_partner(0)
     part_over[PLACE[0, 1]].wait_recv()
     part_over[PLACE[0, 3]].wait_recv()
@@ -489,7 +487,7 @@
             pltpu.VMEM((TOK, W), bf16),
             pltpu.VMEM((TOK, 2 * W), f32),
             pltpu.VMEM((TOK, W), f32),
-            pltpu.VMEM((GROUP, W), bf16),
+            pltpu.VMEM((2 * 2 * ROWS, W), bf16),
             pltpu.VMEM((8, ROWS, D), bf16),
             pltpu.VMEM((2, HALF, X_COLS), bf16),
             pltpu.VMEM((2, 2, HALF, D - X_COLS), bf16),

time: 115 us -> 114 us (level)
    pallas_call x1, Pallas kernels: 113 us -> 112 us  [local(): pl.pallas_call(kernel, out_shape=jax.ShapeDtypeStruct((1, ROWS, D), bf16)...]
where the time goes in v4:
time: 114 us
  Pallas kernels  112 us (98%)
  local copies, waits for them, and re-layouts  1.97 us (2%)
    pallas_call x1, Pallas kernels, local(): pl.pallas_call(kernel, out_shape=jax.ShapeDtypeStruct((1, ROWS, D), bf16)...  112 us

profile of v4, /device:TPU:1, one launch (start us, length us, event | category | flops | bytes accessed | tf_op | source)
XLA Modules:
  0.0 114.0 jit_solution(2362790777454644200)
XLA Ops:
  0.0 112.1 %shard_map.127 = bf16[1,64,5120]{2,1,0:T(8,128)(2,1)} custom-call(bf16[1,64,5120]{2,1,0:T(8,128)(2,1)} %latent_hbm.1, bf16[1,64,5120]{2,1,0:T(8,128)(2,1)} %noise_hbm.1, bf16[1,1024,256]{2,1,0:T(8,128)(2,1)} %ck_hbm.1, bf16[1,1024,256]{2,1,0:T(8,128)(2,1)} %cv_hbm.1, bf16[5120,256]{1,0:T(8,128)(2,1)} %wq_hbm.1, bf16[5120,256]{1,0:T(8,128)(2,1)} %wk_hbm.1, ...), custom_call_target="tpu_custom_call" | custom-call | tf_op jit(solution)/shard_map/pallas_call | solution.py:475
  112.1 2.0 %copy.15 = bf16[1,64,5120]{2,1,0:T(8,128)(2,1)} copy(bf16[1,64,5120]{2,1,0:T(8,128)(2,1)} %shard_map.127) | data formatting | bytes 1310720

commit v5 on v4

--- a/solution.py
+++ b/solution.py
@@ -277,8 +277,8 @@
         loads[name].wait()
     over[0, 0].wait_recv()
     over[1, 0].wait_recv()
+    forward_x(0)
     project(A)
-    forward_x(0)
     over[0, 1].wait_recv()
     over[0, 3].wait_recv()
     project(B)

time: 114 us -> 114 us (level)
  no operation moved by 1% of the time
where the time goes in v5:
time: 114 us
  Pallas kernels  112 us (98%)
  local copies, waits for them, and re-layouts  1.97 us (2%)
    pallas_call x1, Pallas kernels, local(): pl.pallas_call(kernel, out_shape=jax.ShapeDtypeStruct((1, ROWS, D), bf16)...  112 us

profile of v5, /device:TPU:1, one launch (start us, length us, event | category | flops | bytes accessed | tf_op | source)
XLA Modules:
  0.0 114.0 jit_solution(3594552287311156747)
XLA Ops:
  0.0 112.1 %shard_map.127 = bf16[1,64,5120]{2,1,0:T(8,128)(2,1)} custom-call(bf16[1,64,5120]{2,1,0:T(8,128)(2,1)} %latent_hbm.1, bf16[1,64,5120]{2,1,0:T(8,128)(2,1)} %noise_hbm.1, bf16[1,1024,256]{2,1,0:T(8,128)(2,1)} %ck_hbm.1, bf16[1,1024,256]{2,1,0:T(8,128)(2,1)} %cv_hbm.1, bf16[5120,256]{1,0:T(8,128)(2,1)} %wq_hbm.1, bf16[5120,256]{1,0:T(8,128)(2,1)} %wk_hbm.1, ...), custom_call_target="tpu_custom_call" | custom-call | tf_op jit(solution)/shard_map/pallas_call | solution.py:475
  112.1 2.0 %copy.15 = bf16[1,64,5120]{2,1,0:T(8,128)(2,1)} copy(bf16[1,64,5120]{2,1,0:T(8,128)(2,1)} %shard_map.127) | data formatting | bytes 1310720

commit v6 on v5

--- a/solution.py
+++ b/solution.py
@@ -421,10 +421,10 @@
     finish(C, [5, 6, 7])
     part_over[PLACE[0, 2]].wait_recv()
     first_hop(0, PLACE[0, 2], b, r1_b.at[0])
-    finish(B, [5, 6, 7])
     to_partner(1)
     to_partner(3)
     second_hop(1, PLACE[1, 1], PLACE[1, 3], b, r1_b.at[1], r2_b.at[1])
+    finish(B, [5, 6, 7])
     finish(A, [5, 6, 7])
     to_partner(0)
     part_over[PLACE[0, 1]].wait_recv()

time: 114 us -> 114 us (level)
  no operation moved by 1% of the time
where the time goes in v6:
time: 114 us
  Pallas kernels  112 us (98%)
  local copies, waits for them, and re-layouts  1.97 us (2%)
    pallas_call x1, Pallas kernels, local(): pl.pallas_call(kernel, out_shape=jax.ShapeDtypeStruct((1, ROWS, D), bf16)...  112 us

profile of v6, /device:TPU:1, one launch (start us, length us, event | category | flops | bytes accessed | tf_op | source)
XLA Modules:
  0.0 114.0 jit_solution(5873303146778766354)
XLA Ops:
  0.0 112.1 %shard_map.127 = bf16[1,64,5120]{2,1,0:T(8,128)(2,1)} custom-call(bf16[1,64,5120]{2,1,0:T(8,128)(2,1)} %latent_hbm.1, bf16[1,64,5120]{2,1,0:T(8,128)(2,1)} %noise_hbm.1, bf16[1,1024,256]{2,1,0:T(8,128)(2,1)} %ck_hbm.1, bf16[1,1024,256]{2,1,0:T(8,128)(2,1)} %cv_hbm.1, bf16[5120,256]{1,0:T(8,128)(2,1)} %wq_hbm.1, bf16[5120,256]{1,0:T(8,128)(2,1)} %wk_hbm.1, ...), custom_call_target="tpu_custom_call" | custom-call | tf_op jit(solution)/shard_map/pallas_call | solution.py:475
  112.1 2.0 %copy.15 = bf16[1,64,5120]{2,1,0:T(8,128)(2,1)} copy(bf16[1,64,5120]{2,1,0:T(8,128)(2,1)} %shard_map.127) | data formatting | bytes 1310720
